TPU v7x, 256 devices: a whole 4x4x8 slice. The times are simulated.
256 devices in a mesh: zero: 64 (over x, z, core), tensor: 4 (over y).
Axes of the slice: x: 4, y: 4, z: 8, core: 2. Of those that a mesh axis runs over, the one named last changes fastest.
Arguments:
- momentum: bfloat16 [28672, 8192], P('zero', 'tensor'), may hold values from -12 to 12
- gradient: bfloat16 [28672, 8192], P('zero', 'tensor'), may hold values from -12 to 12
- old_basis: bfloat16 [8192, 512], P('tensor'), may hold values from -4 to 4
Outputs:
- new_momentum: bfloat16 [28672, 8192], P('zero', 'tensor')
- new_basis: bfloat16 [8192, 512], P('tensor')
- direction: bfloat16 [28672, 8192], P('zero', 'tensor')
All inputs are finite; a program needn't handle non-finite values.
Results may differ from a plain program's by a relative error of at most 0.023.
Values may be sent and summed in bfloat16 or wider, within the bound.
A program may use at most 64 MiB of HBM per device.

v0:
```python
import math

import jax
import jax.numpy as jnp
from jax import lax
from jax.sharding import PartitionSpec as P

ROWS = 28672
COLS = 8192
RANK = 512


def orthonormalize(projected, gram_sum):
    factor_low = jnp.linalg.cholesky(gram_sum)
    return lax.linalg.triangular_solve(
        factor_low, projected, left_side=False, lower=True, transpose_a=True
    ).astype(jnp.bfloat16)


def per_device(momentum, gradient, old_basis):
    buffer = (momentum.astype(jnp.float32) + gradient.astype(jnp.float32)).astype(jnp.bfloat16)
    projected = lax.psum(
        jnp.dot(buffer, old_basis, preferred_element_type=jnp.float32).astype(jnp.bfloat16),
        "tensor",
    ).astype(jnp.float32)
    gram_sum = lax.psum(jnp.dot(projected.T, projected, precision=lax.Precision.HIGHEST), "zero")
    orthonormal = orthonormalize(projected, gram_sum)
    col_term = lax.dot_general(
        buffer, orthonormal, (((0,), (0,)), ((), ())), preferred_element_type=jnp.float32
    )
    r_whole = lax.psum(col_term, "zero")
    col_squares = lax.psum(jnp.sum(r_whole * r_whole, axis=0), "tensor")
    col_scale = lax.rsqrt(col_squares / COLS + 1e-06)
    r_rounded = r_whole.astype(jnp.bfloat16)
    new_basis = (r_whole * col_scale).astype(jnp.bfloat16)
    low_rank = lax.dot_general(
        orthonormal, r_rounded, (((1,), (1,)), ((), ())), preferred_element_type=jnp.float32
    )
    new_momentum = (buffer.astype(jnp.float32) - 0.05 * low_rank).astype(jnp.bfloat16)
    update = lax.dot_general(
        orthonormal, new_basis, (((1,), (1,)), ((), ())), preferred_element_type=jnp.float32
    )
    direction = (math.sqrt(ROWS / RANK) * update).astype(jnp.bfloat16)
    return (new_momentum, new_basis, direction)


def solution(mesh):
    in_specs = (P("zero", "tensor"), P("zero", "tensor"), P("tensor", None))
    out_specs = (P("zero", "tensor"), P("tensor", None), P("zero", "tensor"))
    return jax.shard_map(
        per_device, mesh=mesh, in_specs=in_specs, out_specs=out_specs, check_vma=False
    )
```

profile of v0, /device:TPU:1, one launch (start us, length us, event | category | flops | bytes accessed | tf_op | source)
XLA Modules:
  0.0 633.2 jit_solution(1119975962977731012)
XLA Ops:
  7.2 1.5 copy-done
  8.8 3.9 convolution_convert_fusion
  12.8 49.7 %all-reduce.5.cloned.1.call-done = bf16[448,512]{1,0:T(8,128)(2,1)} async-done(((bf16[448,512]{1,0:T(8,128)(2,1)}), bf16[448,512]{1,0:T(8,128)(2,1)}) %all-reduce.5.cloned.1.call-update) | async-done | bytes 458768 | tf_op jit(solution)/shard_map/psum | solution.py:22
  62.5 2.7 fusion.35
  65.2 1.0 convert_element_type.36
  66.3 186.8 %all-reduce.7.cloned.1.call-done = f32[512,512]{0,1:T(8,128)} async-done(((f32[512,512]{0,1:T(8,128)}), f32[512,512]{0,1:T(8,128)}) %all-reduce.7.cloned.1.call-update) | async-done | bytes 1048592 | tf_op jit(solution)/shard_map/psum | solution.py:26
  253.1 2.6 copy.7
  255.7 1.4 fusion.1
  257.1 1.0 copy-done.5
  258.1 11.7 %cholesky.104 = f32[128,128]{1,0:T(8,128)S(1)} custom-call(f32[128,128]{1,0:T(8,128)S(1)} %cholesky.266), custom_call_target="Cholesky" | custom-call | tf_op jit(solution)/shard_map/jit(cholesky)/cholesky | solution.py:14
  269.9 9.8 %custom-call.30 = f32[1,128,128]{1,2,0:T(8,128)S(1)} custom-call(f32[1,128,128]{2,1,0:T(8,128)S(1)} %get-tuple-element.30), custom_call_target="InvertDiagBlocksLowerTriangular" | custom-call | tf_op jit(solution)/shard_map/jit(cholesky)/cholesky | solution.py:14
  279.8 1.2 constant_dynamic-update-slice_fusion.3
  281.1 1.3 convolution_subtract_fusion.3
  282.3 11.7 %cholesky.217 = f32[128,128]{1,0:T(8,128)S(1)} custom-call(f32[128,128]{1,0:T(8,128)S(1)} %cholesky.270), custom_call_target="Cholesky" | custom-call | tf_op jit(solution)/shard_map/jit(cholesky)/cholesky | solution.py:14
  294.1 10.0 %custom-call.31 = f32[1,128,128]{1,2,0:T(8,128)S(1)} custom-call(f32[1,128,128]{2,1,0:T(8,128)S(1)} %get-tuple-element.27), custom_call_target="InvertDiagBlocksLowerTriangular" | custom-call | tf_op jit(solution)/shard_map/jit(cholesky)/cholesky | solution.py:14
  304.3 1.3 convolution_subtract_fusion.4
  305.6 11.7 %cholesky.238 = f32[128,128]{1,0:T(8,128)S(1)} custom-call(f32[128,128]{1,0:T(8,128)S(1)} %cholesky.275), custom_call_target="Cholesky" | custom-call | tf_op jit(solution)/shard_map/jit(cholesky)/cholesky | solution.py:14
  317.4 0.7 compare_reduce_fusion.1
  318.1 9.8 %custom-call.32 = f32[1,128,128]{1,2,0:T(8,128)S(1)} custom-call(f32[1,128,128]{2,1,0:T(8,128)S(1)} %get-tuple-element.24), custom_call_target="InvertDiagBlocksLowerTriangular" | custom-call | tf_op jit(solution)/shard_map/jit(cholesky)/cholesky | solution.py:14
  328.1 1.2 convolution_subtract_fusion.5
  329.3 11.7 %cholesky.255 = f32[128,128]{1,0:T(8,128)S(1)} custom-call(f32[128,128]{1,0:T(8,128)S(1)} %convolution_subtract_fusion.5), custom_call_target="Cholesky" | custom-call | tf_op jit(solution)/shard_map/jit(cholesky)/cholesky | solution.py:14
  341.1 0.6 compare_reduce_fusion
  341.7 0.9 compare_reduce_fusion.2
  345.1 1.1 select_select_fusion
  346.2 14.2 %while.1 = (s32[]{:T(128)}, f32[512,512]{1,0:T(8,128)}, s32[4,2]{0,1:T(2,128)S(1)}, f32[4,128,128]{2,1,0:T(8,128)}, s32[]{:T(128)}) while((s32[]{:T(128)}, f32[512,512]{1,0:T(8,128)}, s32[4,2]{0,1:T(2,128)S(1)}, f32[4,128,128]{2,1,0:T(8,128)}, s32[]{:T(128)}) %tuple.34), condition=%wide.while_cond, body=%wide.while_body.sunk | while | flops 2 | bytes 132205 | solution.py:15
  346.3 0.6 fusion.46
  346.9 2.9 bitcast_dynamic-update-slice_fusion.2
  349.9 0.6 fusion.46
  350.5 2.9 bitcast_dynamic-update-slice_fusion.2
  353.4 0.6 fusion.46
  354.0 2.9 bitcast_dynamic-update-slice_fusion.2
  357.0 0.6 fusion.46
  357.6 2.8 bitcast_dynamic-update-slice_fusion.2
  360.4 40.7 %custom-call.33 = f32[4,128,128]{1,2,0:T(8,128)} custom-call(f32[4,128,128]{2,1,0:T(8,128)} %get-tuple-element.10), custom_call_target="InvertDiagBlocksLowerTriangular" | custom-call | tf_op jit(solution)/shard_map/triangular_solve | solution.py:15
  401.1 1.2 fusion.34
  402.3 1.3 convolution_subtract_fusion.2
  403.7 1.3 fusion.33
  405.0 1.4 convolution_subtract_fusion.1
  406.8 1.7 convolution_subtract_fusion
  408.9 3.3 fusion.30
  412.2 193.5 %all-reduce.9.cloned.1.call-done = f32[2048,512]{1,0:T(8,128)} async-done(((f32[2048,512]{1,0:T(8,128)}), f32[2048,512]{1,0:T(8,128)}) %all-reduce.9.cloned.1.call-update) | async-done | bytes 4194320 | tf_op jit(solution)/shard_map/psum | solution.py:31
  605.8 2.5 multiply_reduce_fusion
  608.3 8.4 %psum.31 = f32[512]{0:T(512)S(1)} all-reduce(f32[512]{0:T(512)S(1)} %multiply_reduce_fusion), channel_id=1, replica_groups=mesh['zero'=64,'tensor'=4] {'tensor'}, use_global_device_ids=true, to_apply=%region_12.13 | all-reduce | flops 512 | bytes 4096 | tf_op jit(solution)/shard_map/psum | solution.py:32
  616.8 2.8 multiply_convert_fusion
  619.6 2.4 multiply_convert_fusion.1
  622.0 1.2 copy-done.1
  623.2 0.6 copy-done.8
  624.3 2.4 subtract_convert_fusion
  (46 shorter events, 2.5 us)
Async XLA Ops:
  7.2 1.6 copy-start
  7.2 55.3 %all-reduce.5.cloned.1.call-start = ((), (), s32[]{:S(2)}) async-start(), calls=%async_computation | async-start | bytes 917504 | tf_op jit(solution)/shard_map/psum | solution.py:22
  12.7 240.3 %all-reduce.7.cloned.1.call-start = ((), (), s32[]{:S(2)}) async-start(), calls=%async_computation.1 | async-start | bytes 2097152 | tf_op jit(solution)/shard_map/psum | solution.py:26
  62.5 2.8 copy-start.2
  65.1 540.6 %all-reduce.9.cloned.1.call-start = ((), (), s32[]{:S(2)}) async-start(), calls=%async_computation.2 | async-start | bytes 8388608 | tf_op jit(solution)/shard_map/psum | solution.py:31
  253.1 2.6 copy-start.3
  257.1 1.0 copy-start.5
  346.2 58.8 %copy-start.4 = (f32[448,512]{1,0:T(8,128)S(1)}, f32[448,512]{1,0:T(8,128)}, u32[]{:S(2)}) copy-start(f32[448,512]{1,0:T(8,128)} %convert_element_type.36) | copy-start | bytes 2752516
  401.1 5.3 copy-start.11
  403.7 5.2 copy-start.7
  403.7 5.2 copy-start.9
  619.5 2.4 copy-start.6
  619.5 3.6 copy-start.1
  619.6 4.2 copy-start.8
  619.6 4.7 copy-start.10
Sparse Core Ops, SparseCore 0:
  12.8 49.5 all-reduce.4
  66.8 186.1 all-reduce.6
  412.4 193.3 all-reduce.8
where the time goes:
time: 636 us; the launch traced here: 633 us
  waiting for transfers between devices  430 us (68%)
  other arithmetic  128 us (20%)
  matrix products  27.8 us (4%)
  local copies, waits for them, and re-layouts  21.8 us (3%)
  between operations  16.6 us (3%)
  blocking collectives  8.45 us (1%)
    psum x1, waiting for transfers between devices, per_device(): r_whole = lax.psum(col_term, 'zero')  194 us
    psum x1, waiting for transfers between devices, per_device(): lax.psum(jnp.dot(projected.T, projected, precision=lax.Precision.HIGHEST)...  187 us
    another operation x14, other arithmetic, orthonormalize(): factor_low = jnp.linalg.cholesky(gram_sum)  78.8 us
    psum x1, waiting for transfers between devices, per_device(): lax.psum(jnp.dot(buffer, old_basis, preferred_element_type=jnp.float32).a...  49.7 us
    another operation x3, other arithmetic, orthonormalize(): lax.linalg.triangular_solve(factor_low, projected, left_side=False, lower...  41.8 us
    another operation x12, local copies, waits for them, and re-layouts  14.1 us
  transfers between devices with their start and end apart: 3, of which 3 were waited for; matrix products, arithmetic and copies ran while one was open for 0% of the time, Pallas kernels for 0%

commit v1 on v0

v1 whole, which is shorter than its diff:
```python
import functools
import math

import jax
import jax.numpy as jnp
from jax import lax
from jax.experimental import pallas as pl
from jax.experimental.pallas import tpu as pltpu
from jax.sharding import PartitionSpec as P

ROWS = 28672
COLS = 8192
RANK = 512
F32 = jnp.float32
BF16 = jnp.bfloat16
HIGHEST = lax.Precision.HIGHEST
SHAPE = (4, 8, 4)
VMEM_LIMIT = 56 * 1024 * 1024


def dot(a, b, contract=((1,), (0,)), precision=None):
    return lax.dot_general(
        a, b, (contract, ((), ())), precision=precision, preferred_element_type=F32
    )


def reduce_kernel(shape, mom, grad, basis, p_out, g_out, t_out, buf, p_part, p_rx, p_t,
                  g_send, g_own, g_core, g_xs, g_xrx, g_zs, g_zrx,
                  t_send, t_own, t_core, t_xs, t_xrx, t_zs, t_zrx,
                  core_s, core_r, x_s, x_r, y_s, y_r, z_s, z_r):
    nx, nz, ny = shape
    zero, y = lax.axis_index("zero"), lax.axis_index("tensor")
    c = lax.rem(zero, 2)
    z = lax.rem(lax.div(zero, 2), nz)
    x = lax.div(zero, 2 * nz)
    other = 1 - c

    def at(xx, zz, cc):
        return (xx * nz + zz) * 2 + cc

    def hop(axis, d):
        if axis == "x":
            return (at(lax.rem(x + d, nx), z, c), y)
        if axis == "z":
            return (at(x, lax.rem(z + d, nz), c), y)
        if axis == "y":
            return (zero, lax.rem(y + d, ny))
        return (at(x, z, other), y)

    def copy(src, dst, send, recv, device):
        return pltpu.make_async_remote_copy(
            src_ref=src, dst_ref=dst, send_sem=send, recv_sem=recv,
            device_id=device, device_id_type=pl.DeviceIdType.MESH)

    barrier = pltpu.get_barrier_semaphore()
    peers = [hop("y", d) for d in range(1, ny)] + [hop("x", d) for d in range(1, nx)]
    peers += [hop("z", d) for d in range(1, nz)] + [hop("core", 1)]
    for peer in peers:
        pl.semaphore_signal(barrier, inc=1, device_id=peer, device_id_type=pl.DeviceIdType.MESH)

    pending = []

    def partial_rows(u):
        rows = (mom[u].astype(F32) + grad[u].astype(F32)).astype(BF16)
        buf[u] = rows
        return dot(rows, basis[...])

    order = sorted(range(1, ny), key=lambda d: -min(d, ny - d))
    started = {}
    for n, d in enumerate(order):
        u = lax.rem(y + d, ny)
        p_part[d - 1] = partial_rows(u).astype(BF16)
        if n == 0:
            pl.semaphore_wait(barrier, len(peers))
        started[d] = copy(p_part.at[d - 1], p_rx.at[d - 1], y_s.at[0, d - 1], y_r.at[0, d - 1], hop("y", d))
        started[d].start()
    own = partial_rows(y)
    for d in order:
        started[d].wait_recv()
        own = own + p_rx[d - 1].astype(F32)
    p_out[y] = own.astype(BF16)
    pending += started.values()
    gathers = []
    for d in order:
        go = copy(p_out.at[y], p_out.at[y], y_s.at[1, d - 1], y_r.at[1, d - 1], hop("y", d))
        go.start()
        gathers.append(go)

    def finish_gather(axis, n, view, copies, sems):
        me, size = {"x": (x, nx), "y": (y, ny), "z": (z, nz)}[axis]
        for d in range(1, size):
            src = lax.rem(me - d + size, size)
            copy(view(src), view(src), sems[0].at[n, d - 1], sems[1].at[n, d - 1], hop(axis, d)).wait_recv()
        pending.extend(copies)

    def start_gather(axis, n, view, sems):
        me, size = {"x": (x, nx), "y": (y, ny), "z": (z, nz)}[axis]
        copies = []
        for d in sorted(range(1, size), key=lambda d: -min(d, size - d)):
            go = copy(view(me), view(me), sems[0].at[n, d - 1], sems[1].at[n, d - 1], hop(axis, d))
            go.start()
            copies.append(go)
        return copies

    def start_scatter(axis, n, send, rx, sems):
        me, size = {"x": (x, nx), "y": (y, ny), "z": (z, nz)}[axis]
        copies = []
        for d in sorted(range(1, size), key=lambda d: -min(d, size - d)):
            go = copy(send.at[lax.rem(me + d, size)], rx.at[d - 1], sems[0].at[n, d - 1], sems[1].at[n, d - 1], hop(axis, d))
            go.start()
            copies.append(go)
        return copies

    def end_scatter(copies):
        for go in copies:
            go.wait_recv()
        pending.extend(copies)

    xs, ys, zs = (x_s, x_r), (y_s, y_r), (z_s, z_r)
    finish_gather("y", 1, lambda i: p_out.at[i], gathers, ys)

    rows, rank = buf.shape[0] * buf.shape[1], p_out.shape[2]
    half = rank // 2
    p_all = p_out[...].reshape(rows, rank)
    p_t[...] = p_all.T.reshape(2, half, rows)
    gcols = rank // ny

    p_cols = [p_all[:, gcols * i: gcols * (i + 1)] for i in range(ny)]
    p_mine = p_cols[0]
    for i in range(1, ny):
        p_mine = jnp.where(y == i, p_cols[i], p_mine)
    g_send[...] = dot(p_t[other], p_mine).reshape(g_send.shape)
    g_go = copy(g_send, g_core, core_s.at[0], core_r.at[0], hop("core", 1))
    g_go.start()
    g_own[...] = dot(p_t[c], p_mine).reshape(g_own.shape)

    cb = t_send.shape[3]
    for k in range(nz):
        cols = buf[:, :, cb * k: cb * (k + 1)].reshape(rows, cb)
        t_send[:, k] = dot(p_t[other], cols).astype(BF16).reshape(t_send.shape[0], t_send.shape[2], cb)
    t_go = []
    for i in range(nx):
        go = copy(t_send.at[i], t_core.at[i], core_s.at[1 + i], core_r.at[1 + i], hop("core", 1))
        go.start()
        t_go.append(go)
    for k in range(nz):
        cols = buf[:, :, cb * k: cb * (k + 1)].reshape(rows, cb)
        t_own[:, k] = dot(p_t[c], cols).reshape(t_send.shape[0], t_send.shape[2], cb)

    g_go.wait_recv()
    g_xs[...] = g_own[...] + g_core[...]
    g_x = start_scatter("x", 0, g_xs, g_xrx, xs)
    for i in range(nx):
        t_go[i].wait_recv()
    pending += [g_go, *t_go]

    def add_core(i, carry):
        total = t_own[i] + t_core[i].astype(F32)
        t_own[i] = total
        t_xs[i] = total.astype(BF16)
        return carry

    lax.fori_loop(0, nx, add_core, 0)
    t_x = start_scatter("x", 1, t_xs, t_xrx, xs)

    end_scatter(g_x)
    g_zs[...] = sum((g_xrx[d] for d in range(nx - 1)), g_xs[x])
    g_z = start_scatter("z", 0, g_zs, g_zrx, zs)
    end_scatter(t_x)

    def add_x(k, carry):
        total = t_own[x, k]
        for d in range(nx - 1):
            total = total + t_xrx[d, k].astype(F32)
        t_own[x, k] = total
        t_zs[k] = total.astype(BF16)
        return carry

    lax.fori_loop(0, nz, add_x, 0)
    t_z = start_scatter("z", 1, t_zs, t_zrx, zs)

    end_scatter(g_z)
    g_out[c, x, y, z] = sum((g_zrx[d] for d in range(nz - 1)), g_zs[z])
    g_gz = start_gather("z", 2, lambda i: g_out.at[c, x, y, i], zs)
    end_scatter(t_z)
    t_out[c, x, z] = sum((t_zrx[d].astype(F32) for d in range(nz - 1)), t_own[x, z]).astype(BF16)
    t_gz = start_gather("z", 3, lambda i: t_out.at[c, x, i], zs)

    finish_gather("z", 2, lambda i: g_out.at[c, x, y, i], g_gz, zs)
    g_gy = start_gather("y", 2, lambda i: g_out.at[c, x, i], ys)
    finish_gather("z", 3, lambda i: t_out.at[c, x, i], t_gz, zs)
    t_gx = start_gather("x", 2, lambda i: t_out.at[c, i], xs)
    finish_gather("y", 2, lambda i: g_out.at[c, x, i], g_gy, ys)
    g_gx = start_gather("x", 3, lambda i: g_out.at[c, i], xs)
    finish_gather("x", 2, lambda i: t_out.at[c, i], t_gx, xs)
    t_gc = copy(t_out.at[c], t_out.at[c], core_s.at[nx + 1], core_r.at[nx + 1], hop("core", 1))
    t_gc.start()
    finish_gather("x", 3, lambda i: g_out.at[c, i], g_gx, xs)
    g_gc = copy(g_out.at[c], g_out.at[c], core_s.at[nx + 2], core_r.at[nx + 2], hop("core", 1))
    g_gc.start()
    copy(t_out.at[other], t_out.at[other], core_s.at[nx + 1], core_r.at[nx + 1], hop("core", 1)).wait_recv()
    copy(g_out.at[other], g_out.at[other], core_s.at[nx + 2], core_r.at[nx + 2], hop("core", 1)).wait_recv()
    pending += [t_gc, g_gc]
    for go in pending:
        go.wait_send()


def reduce_call(shape, mom, grad, basis):
    nx, nz, ny = shape
    rows, cols = mom.shape
    rank = basis.shape[1]
    part, cb, rb, gb = rows // ny, cols // nz, rank // (2 * nx), rank // (2 * nx * nz)
    gc = rank // ny
    vmem, sem = pltpu.VMEM, pltpu.SemaphoreType.DMA
    space = pl.BlockSpec(memory_space=pltpu.VMEM)
    return pl.pallas_call(
        functools.partial(reduce_kernel, shape),
        out_shape=(
            jax.ShapeDtypeStruct((ny, part, rank), BF16),
            jax.ShapeDtypeStruct((2, nx, ny, nz, gb, gc), F32),
            jax.ShapeDtypeStruct((2, nx, nz, rb, cb), BF16),
        ),
        in_specs=[space] * 3,
        out_specs=(space,) * 3,
        scratch_shapes=[
            vmem((ny, part, cols), BF16),
            vmem((ny - 1, part, rank), BF16),
            vmem((ny - 1, part, rank), BF16),
            vmem((2, rank // 2, rows), BF16),
            vmem((nx, nz, gb, gc), F32),
            vmem((nx, nz, gb, gc), F32),
            vmem((nx, nz, gb, gc), F32),
            vmem((nx, nz, gb, gc), F32),
            vmem((nx - 1, nz, gb, gc), F32),
            vmem((nz, gb, gc), F32),
            vmem((nz - 1, gb, gc), F32),
            vmem((nx, nz, rb, cb), BF16),
            vmem((nx, nz, rb, cb), F32),
            vmem((nx, nz, rb, cb), BF16),
            vmem((nx, nz, rb, cb), BF16),
            vmem((nx - 1, nz, rb, cb), BF16),
            vmem((nz, rb, cb), BF16),
            vmem((nz - 1, rb, cb), BF16),
            sem((nx + 3,)), sem((nx + 3,)),
            sem((4, nx - 1)), sem((4, nx - 1)),
            sem((3, ny - 1)), sem((3, ny - 1)),
            sem((4, nz - 1)), sem((4, nz - 1)),
        ],
        compiler_params=pltpu.CompilerParams(
            collective_id=0, has_side_effects=True, vmem_limit_bytes=VMEM_LIMIT),
        name="reduce",
    )(mom.reshape(ny, part, cols), grad.reshape(ny, part, cols), basis)


def factor8(cols):
    e = [[jnp.broadcast_to(cols[k][q:q + 1, :], (8, 128)) for k in range(q + 1)] for q in range(8)]
    low = [[None] * 8 for _ in range(8)]
    inv = [[None] * 8 for _ in range(8)]
    for p in range(8):
        inv[p][p] = lax.rsqrt(e[p][p])
        for q in range(p + 1, 8):
            low[q][p] = e[q][p] * inv[p][p]
        for q in range(p + 1, 8):
            for k in range(p + 1, q + 1):
                e[q][k] = e[q][k] - low[q][p] * low[k][p]
    for q in range(8):
        for k in range(q):
            acc = low[q][k] * inv[k][k]
            for m in range(k + 1, q):
                acc = acc + low[q][m] * inv[m][k]
            inv[q][k] = -acc * inv[q][q]
    return inv


def lanes(x, k):
    return jnp.broadcast_to(x[:, k:k + 1], (8, 128))


def rows8(x, k):
    return jnp.broadcast_to(x[k:k + 1, :], (8, 128))


def factor128(r):
    sub = lax.broadcasted_iota(jnp.int32, (8, 128), 0)
    for s in range(16):
        lo = 8 * s
        a, v = r[lo:lo + 8, 0:128], r[lo:lo + 8, 128:256]
        cols = [lanes(a, lo + k) for k in range(8)]
        if s < 15:
            an, vn = r[lo + 8:lo + 16, 0:128], r[lo + 8:lo + 16, 128:256]
            nxt = [lanes(an, lo + k) for k in range(8)]
        inv = factor8(cols)
        new_a = new_v = None
        for k in range(8):
            m = jnp.where(sub == k, inv[k][k], 0.0)
            for q in range(k + 1, 8):
                m = jnp.where(sub == q, inv[q][k], m)
            ta, tv = m * rows8(a, k), m * rows8(v, k)
            new_a = ta if new_a is None else new_a + ta
            new_v = tv if new_v is None else new_v + tv
        r[lo:lo + 8, 128:256] = new_v
        if s < 15:
            for k in range(8):
                lc = nxt[0] * inv[k][0]
                for j in range(1, k + 1):
                    lc = lc + nxt[j] * inv[k][j]
                an = an - lc * rows8(new_a, k)
                vn = vn - lc * rows8(new_v, k)
            r[lo + 8:lo + 16, 0:128], r[lo + 8:lo + 16, 128:256] = an, vn
        if s < 14:
            both = jnp.concatenate([new_a, new_v], axis=1)
            update = dot(new_a, both, ((0,), (0,)), HIGHEST)
            r[lo + 16:128, :] = r[lo + 16:128, :] - update[lo + 16:128, :]


def split(x):
    high = x.astype(BF16)
    return high, (x - high.astype(F32)).astype(BF16)


def factor_kernel(p_ref, g_ref, t_ref, orth_ref, r_ref, sq_ref, m, w):
    rank = m.shape[0]
    nb = rank // 128
    for i in range(2):
        for j in range(g_ref.shape[1]):
            for k in range(g_ref.shape[2]):
                rows = g_ref.shape[3] * g_ref.shape[4]
                lo = (i * g_ref.shape[1] + j) * rows
                m[lo:lo + rows, 128 * k:128 * (k + 1)] = g_ref[i, j, k].reshape(rows, 128)
    row = lax.broadcasted_iota(jnp.int32, (128, 128), 0)
    col = lax.broadcasted_iota(jnp.int32, (128, 128), 1)
    eye = jnp.where(row == col, 1.0, 0.0)
    for i in range(nb):
        for j in range(nb):
            m[128 * i:128 * (i + 1), rank + 128 * j:rank + 128 * (j + 1)] = eye if i == j else jnp.zeros_like(eye)
    for k in range(nb):
        lo, hi = 128 * k, 128 * (k + 1)
        w[:, 0:128] = m[lo:hi, lo:hi]
        w[:, 128:256] = eye
        factor128(w)
        inv = w[:, 128:256]
        m[lo:hi, hi:rank + hi] = dot(inv, m[lo:hi, hi:rank + hi], precision=HIGHEST)
        if k + 1 < nb:
            m[hi:, hi:rank + hi] = m[hi:, hi:rank + hi] - dot(
                m[lo:hi, hi:rank], m[lo:hi, hi:rank + hi], ((0,), (0,)), HIGHEST)
    high, low = split(m[:, rank:])
    rows = p_ref.shape[0] * p_ref.shape[1]
    p_all = p_ref[...].reshape(rows, rank)
    orth_ref[...] = (dot(p_all, high, ((1,), (1,))) + dot(p_all, low, ((1,), (1,)))).astype(BF16)
    nz, cb = t_ref.shape[2], t_ref.shape[4]
    total = jnp.zeros((rank, 128), F32)
    for k in range(nz):
        t = t_ref[:, :, k].reshape(rank, cb)
        r = dot(high, t) + dot(low, t)
        r_ref[:, cb * k:cb * (k + 1)] = r
        sq = r * r
        for i in range(cb // 128):
            total = total + sq[:, 128 * i:128 * (i + 1)]
    sq_ref[...] = jnp.sum(total, axis=1, keepdims=True)


def factor_call(p_sum, gram, t_sum):
    rows, rank = p_sum.shape[0] * p_sum.shape[1], p_sum.shape[2]
    cols = t_sum.shape[2] * t_sum.shape[4]
    space = pl.BlockSpec(memory_space=pltpu.VMEM)
    return pl.pallas_call(
        factor_kernel,
        out_shape=(
            jax.ShapeDtypeStruct((rows, rank), BF16),
            jax.ShapeDtypeStruct((rank, cols), F32),
            jax.ShapeDtypeStruct((rank, 1), F32),
        ),
        in_specs=[space] * 3,
        out_specs=(space,) * 3,
        scratch_shapes=[pltpu.VMEM((rank, 2 * rank), F32), pltpu.VMEM((128, 256), F32)],
        compiler_params=pltpu.CompilerParams(vmem_limit_bytes=VMEM_LIMIT),
        name="factor",
    )(p_sum, gram, t_sum)


def per_device(momentum, gradient, old_basis):
    p_sum, gram, t_sum = reduce_call(SHAPE, momentum, gradient, old_basis)
    orthonormal, r_t, squares = factor_call(p_sum, gram, t_sum)
    col_squares = lax.psum(squares, "tensor")
    col_scale = lax.rsqrt(col_squares / COLS + 1e-06)
    buffer = (momentum.astype(F32) + gradient.astype(F32)).astype(BF16)
    low_rank = dot(orthonormal, r_t.astype(BF16))
    new_momentum = (buffer.astype(F32) - 0.05 * low_rank).astype(BF16)
    basis_t = (r_t * col_scale).astype(BF16)
    direction = (math.sqrt(ROWS / RANK) * dot(orthonormal, basis_t)).astype(BF16)
    return (new_momentum, basis_t.T, direction)


def solution(mesh):
    in_specs = (P("zero", "tensor"), P("zero", "tensor"), P("tensor", None))
    out_specs = (P("zero", "tensor"), P("tensor", None), P("zero", "tensor"))
    return jax.shard_map(
        per_device, mesh=mesh, in_specs=in_specs, out_specs=out_specs, check_vma=False
    )
```

time: 636 us -> 146 us (0.23)
  waiting for transfers between devices: 430 us -> 0 us
  other arithmetic: 128 us -> 0.43 us
  Pallas kernels: 0 us -> 115 us
  matrix products: 27.8 us -> 7.3 us
  local copies, waits for them, and re-layouts: 21.8 us -> 2.53 us
  between operations: 16.6 us -> 0.7 us
  blocking collectives: 8.45 us -> 17.7 us
    psum x3 -> x0, waiting for transfers between devices: 430 us -> none  [the longest x1 194 us: per_device(): r_whole = lax.psum(col_term, 'zero')]
    another operation x17 -> x0, other arithmetic: 121 us -> none  [the longest x14 78.8 us: orthonormalize(): factor_low = jnp.linalg.cholesky(gram_sum)]
    pallas_call x0 -> x2, Pallas kernels: none -> 115 us  [the longest x1 82.7 us: reduce_call(): pl.pallas_call(functools.partial(reduce_kernel, shape), out_shape=(jax.Sh...]
    another operation x17 -> x0, local copies, waits for them, and re-layouts: 14.3 us -> none
    another operation x13 -> x0, matrix products: 13.1 us -> none  [the longest x7 7.61 us: orthonormalize(): lax.linalg.triangular_solve(factor_low, projected, left_side=False, lower...]
    psum x1, blocking collectives: 8.45 us -> 17.7 us  [per_device(): col_squares = lax.psum(squares, 'tensor')]
    dot_general x5 -> x2, matrix products: 14.7 us -> 7.3 us  [dot(): lax.dot_general(a, b, (contract, ((), ())), precision=precision, preferre...]
  transfers between devices with their start and end apart: 3 -> 0, of which waited for: 3 -> 0; matrix products, arithmetic and copies ran while one was open for 0% -> 0% of each run, Pallas kernels for 0% -> 0%
where the time goes in v1:
time: 146 us; the launch traced here: 144 us
  Pallas kernels  115 us (79%)
  blocking collectives  17.7 us (12%)
  matrix products  7.3 us (5%)
  local copies, waits for them, and re-layouts  2.53 us (2%)
    pallas_call x1, Pallas kernels, reduce_call(): pl.pallas_call(functools.partial(reduce_kernel, shape), out_shape=(jax.Sh...  82.7 us
    pallas_call x1, Pallas kernels, factor_call(): pl.pallas_call(factor_kernel, out_shape=(jax.ShapeDtypeStruct((rows, rank...  32.2 us
    psum x1, blocking collectives, per_device(): col_squares = lax.psum(squares, 'tensor')  17.7 us
    dot_general x2, matrix products, dot(): lax.dot_general(a, b, (contract, ((), ())), precision=precision, preferre...  7.3 us

profile of v1, /device:TPU:1, one launch (start us, length us, event | category | flops | bytes accessed | tf_op | source)
XLA Modules:
  0.0 143.6 jit_solution(6853796965707564891)
XLA Ops:
  0.6 82.7 %reduce.3 = (bf16[4,112,512]{2,1,0:T(8,128)(2,1)}, f32[2,4,4,8,8,128]{5,4,3,2,1,0:T(8,128)}, bf16[2,4,8,64,256]{4,3,2,1,0:T(8,128)(2,1)}) custom-call(bf16[4,112,2048]{2,1,0:T(8,128)(2,1)} %bitcast.6, bf16[4,112,2048]{2,1,0:T(8,128)(2,1)} %bitcast.7, bf16[2048,512]{1,0:T(8,128)(2,1)} %basis.1), custom_call_target="tpu_custom_call" | custom-call | tf_op jit(solution)/shard_map/reduce/pallas_call | solution.py:216
  83.3 32.2 %factor.1 = (bf16[448,512]{1,0:T(8,128)(2,1)}, f32[512,2048]{1,0:T(8,128)}, f32[512,1]{1,0:T(8,128)}) custom-call(bf16[4,112,512]{2,1,0:T(8,128)(2,1)} %get-tuple-element.9.p_ref, f32[2,4,4,8,8,128]{5,4,3,2,1,0:T(8,128)} %get-tuple-element.10.g_ref, bf16[2,4,8,64,256]{4,3,2,1,0:T(8,128)(2,1)} %get-tuple-element.11.t_ref), custom_call_target="tpu_custom_call" | custom-call | tf_op jit(solution)/shard_map/factor/pallas_call | solution.py:366
  115.5 17.7 %psum.7 = f32[512,1]{1,0:T(8,128)S(1)} all-reduce(f32[512,1]{1,0:T(8,128)} %get-tuple-element.14), channel_id=1, replica_groups=mesh['zero'=64,'tensor'=4] {'tensor'}, use_global_device_ids=true, to_apply=%region_0.0 | all-reduce | flops 512 | bytes 4096 | tf_op jit(solution)/shard_map/psum | solution.py:384
  133.3 0.2 rsqrt_reduce_fusion
  133.4 0.0 copy-start
  133.5 0.0 copy-start.1
  133.5 0.0 copy-start.2
  133.5 0.0 copy-start.3
  133.5 4.9 %multiply_convert_fusion.1 = bf16[448,2048]{1,0:T(8,128)(2,1)} fusion(bf16[448,512]{1,0:T(8,128)(2,1)} %get-tuple-element.12, f32[512,2048]{1,0:T(8,128)} %get-tuple-element.13, f32[512]{0:T(512)S(1)} %rsqrt_reduce_fusion), kind=kOutput, calls=%fused_computation.1 | convolution fusion | flops 943456256 | bytes 6490112 | tf_op jit(solution)/shard_map/dot_general | solution.py:22
  138.4 0.0 copy-done
  138.4 0.0 copy-done.1
  138.4 0.0 copy-done.2
  138.4 0.0 copy-done.3
  138.4 2.4 %subtract_convert_fusion = bf16[448,2048]{1,0:T(8,128)(2,1)} fusion(bf16[448,512]{1,0:T(8,128)(2,1)S(1)} %copy-done.3, f32[512,2048]{1,0:T(8,128)S(1)} %copy-done, bf16[448,2048]{1,0:T(8,128)(2,1)S(1)} %copy-done.2, bf16[448,2048]{1,0:T(8,128)(2,1)S(1)} %copy-done.1), kind=kOutput, calls=%fused_computation.2 | convolution fusion | flops 947912704 | bytes 10158080 | tf_op jit(solution)/shard_map/dot_general | solution.py:22
  140.8 0.3 fusion.1
  141.1 2.5 %copy.7 = bf16[2048,512]{1,0:T(8,128)(2,1)} copy(bf16[2048,512]{0,1:T(8,128)(2,1)S(1)} %fusion.1) | data formatting | bytes 4194304
Async XLA Ops:
  133.4 5.0 %copy-start = (f32[512,2048]{1,0:T(8,128)S(1)}, f32[512,2048]{1,0:T(8,128)}, u32[]{:S(2)}) copy-start(f32[512,2048]{1,0:T(8,128)} %get-tuple-element.13) | copy-start | bytes 12582916
  133.5 5.0 %copy-start.1 = (bf16[448,2048]{1,0:T(8,128)(2,1)S(1)}, bf16[448,2048]{1,0:T(8,128)(2,1)}, u32[]{:S(2)}) copy-start(bf16[448,2048]{1,0:T(8,128)(2,1)} %param.3) | copy-start | bytes 5505028
  133.5 4.9 %copy-start.2 = (bf16[448,2048]{1,0:T(8,128)(2,1)S(1)}, bf16[448,2048]{1,0:T(8,128)(2,1)}, u32[]{:S(2)}) copy-start(bf16[448,2048]{1,0:T(8,128)(2,1)} %param.4) | copy-start | bytes 5505028
  133.5 4.9 %copy-start.3 = (bf16[448,512]{1,0:T(8,128)(2,1)S(1)}, bf16[448,512]{1,0:T(8,128)(2,1)}, u32[]{:S(2)}) copy-start(bf16[448,512]{1,0:T(8,128)(2,1)} %get-tuple-element.12) | copy-start | bytes 1376260

commit v2 on v1

v2 whole, which is shorter than its diff:
```python
import functools
import math

import jax
import jax.numpy as jnp
from jax import lax
from jax.experimental import pallas as pl
from jax.experimental.pallas import tpu as pltpu
from jax.sharding import PartitionSpec as P

ROWS = 28672
COLS = 8192
RANK = 512
F32 = jnp.float32
BF16 = jnp.bfloat16
HIGHEST = lax.Precision.HIGHEST
SHAPE = (4, 8, 4)
VMEM_LIMIT = 56 * 1024 * 1024


def dot(a, b, contract=((1,), (0,)), precision=None):
    return lax.dot_general(
        a, b, (contract, ((), ())), precision=precision, preferred_element_type=F32
    )


def update_kernel(shape, cols_total, mom_hbm, grad_hbm, basis_hbm, orth_ref, r_ref, nb_ref, buf,
                  mom, grad, basis, p_part, p_rx, p_sum, p_t,
                  g_send, g_own, g_core, g_xs, g_xrx, g_zs, g_zrx, g_all,
                  t_send, t_own, t_core, t_xs, t_xrx, t_zs, t_zrx, t_all,
                  m, w, sq_own, sq_rx, in_s, core_s, core_r, x_s, x_r, y_s, y_r, z_s, z_r, xy_s, xy_r):
    nx, nz, ny = shape
    zero, y = lax.axis_index("zero"), lax.axis_index("tensor")
    c = lax.rem(zero, 2)
    z = lax.rem(lax.div(zero, 2), nz)
    x = lax.div(zero, 2 * nz)
    other = 1 - c

    def at(xx, zz, cc):
        return (xx * nz + zz) * 2 + cc

    def hop(axis, d):
        if axis == "x":
            return (at(lax.rem(x + d, nx), z, c), y)
        if axis == "z":
            return (at(x, lax.rem(z + d, nz), c), y)
        if axis == "y":
            return (zero, lax.rem(y + d, ny))
        if axis == "xy":
            return (at(lax.rem(x + d[0], nx), z, c), lax.rem(y + d[1], ny))
        return (at(x, z, other), y)

    def copy(src, dst, send, recv, device):
        return pltpu.make_async_remote_copy(
            src_ref=src, dst_ref=dst, send_sem=send, recv_sem=recv,
            device_id=device, device_id_type=pl.DeviceIdType.MESH)

    def far_first(size):
        return sorted(range(1, size), key=lambda d: -min(d, size - d))

    plane = [(i, j) for i in range(nx) for j in range(ny) if i or j]
    plane.sort(key=lambda d: -(min(d[0], nx - d[0]) + min(d[1], ny - d[1])))
    barrier = pltpu.get_barrier_semaphore()
    peers = [hop("xy", d) for d in plane] + [hop("z", d) for d in range(1, nz)] + [hop("core", 1)]
    for peer in peers:
        pl.semaphore_signal(barrier, inc=1, device_id=peer, device_id_type=pl.DeviceIdType.MESH)

    y_order = far_first(ny) + [0]
    loads = {}
    for n, d in enumerate(y_order):
        u = lax.rem(y + d, ny)
        loads[d] = [
            pltpu.make_async_copy(mom_hbm.at[u], mom.at[d], in_s.at[0, d]),
            pltpu.make_async_copy(grad_hbm.at[u], grad.at[d], in_s.at[1, d]),
        ]
        for go in loads[d]:
            go.start()
        if n == 0:
            load_basis = pltpu.make_async_copy(basis_hbm, basis, in_s.at[2, 0])
            load_basis.start()
    load_basis_wait = [load_basis]

    pending = []

    def partial_rows(d):
        for go in loads[d] + load_basis_wait:
            go.wait()
        load_basis_wait.clear()
        rows = (mom[d].astype(F32) + grad[d].astype(F32)).astype(BF16)
        buf[lax.rem(y + d, ny)] = rows
        return dot(rows, basis[...])

    def start_scatter(axis, n, send, rx, sems):
        me, size = {"x": (x, nx), "y": (y, ny), "z": (z, nz)}[axis]
        copies = []
        for d in far_first(size):
            src = send.at[lax.rem(me + d, size)]
            go = copy(src, rx.at[d - 1], sems[0].at[n, d - 1], sems[1].at[n, d - 1], hop(axis, d))
            go.start()
            copies.append(go)
        return copies

    def start_exchange(axis, n, send, rx, sems):
        size = {"x": nx, "y": ny, "z": nz}[axis]
        copies = []
        for d in far_first(size):
            go = copy(send, rx.at[d - 1], sems[0].at[n, d - 1], sems[1].at[n, d - 1], hop(axis, d))
            go.start()
            copies.append(go)
        return copies

    def arrived(copies):
        for go in copies:
            go.wait_recv()
        pending.extend(copies)

    def start_gather(axis, n, view, sems):
        me, size = {"x": (x, nx), "y": (y, ny), "z": (z, nz)}[axis]
        copies = []
        for d in far_first(size):
            go = copy(view(me), view(me), sems[0].at[n, d - 1], sems[1].at[n, d - 1], hop(axis, d))
            go.start()
            copies.append(go)
        return copies

    def gathered(axis, n, view, copies, sems):
        me, size = {"x": (x, nx), "y": (y, ny), "z": (z, nz)}[axis]
        for d in far_first(size):
            src = lax.rem(me - d + size, size)
            copy(view(src), view(src), sems[0].at[n, d - 1], sems[1].at[n, d - 1], hop(axis, d)).wait_recv()
        pending.extend(copies)

    xs, ys, zs = (x_s, x_r), (y_s, y_r), (z_s, z_r)

    for d in y_order[:-1]:
        p_part[d - 1] = partial_rows(d).astype(BF16)
    pl.semaphore_wait(barrier, len(peers))
    p_go = []
    for d in y_order[:-1]:
        go = copy(p_part.at[d - 1], p_rx.at[d - 1], y_s.at[0, d - 1], y_r.at[0, d - 1], hop("y", d))
        go.start()
        p_go.append(go)
    own = partial_rows(0)
    for d, go in zip(y_order, p_go):
        go.wait_recv()
        own = own + p_rx[d - 1].astype(F32)
    p_sum[y] = own.astype(BF16)
    pending += p_go
    p_go = start_gather("y", 1, lambda i: p_sum.at[i], ys)
    gathered("y", 1, lambda i: p_sum.at[i], p_go, ys)

    rows, rank = buf.shape[0] * buf.shape[1], p_sum.shape[2]
    half = rank // 2
    p_all = p_sum[...].reshape(rows, rank)
    p_t[...] = p_all.T.reshape(2, half, rows)
    gcols = rank // ny

    p_cols = [p_all[:, gcols * i: gcols * (i + 1)] for i in range(ny)]
    p_mine = p_cols[0]
    for i in range(1, ny):
        p_mine = jnp.where(y == i, p_cols[i], p_mine)
    g_send[...] = dot(p_t[other], p_mine).reshape(g_send.shape)
    g_go = copy(g_send, g_core, core_s.at[0], core_r.at[0], hop("core", 1))
    g_go.start()
    g_own[...] = dot(p_t[c], p_mine).reshape(g_own.shape)
    arrived([g_go])
    g_xs[...] = g_own[...] + g_core[...]
    g_x = start_scatter("x", 0, g_xs, g_xrx, xs)

    cb = t_send.shape[3]
    t_shape = (t_send.shape[0], t_send.shape[2], cb)
    for k in range(nz):
        cols = buf[:, :, cb * k: cb * (k + 1)].reshape(rows, cb)
        t_send[:, k] = dot(p_t[other], cols).astype(BF16).reshape(t_shape)
    t_go = []
    for i in range(nx):
        go = copy(t_send.at[i], t_core.at[i], core_s.at[1 + i], core_r.at[1 + i], hop("core", 1))
        go.start()
        t_go.append(go)
    arrived(g_x)
    g_zs[...] = sum((g_xrx[d] for d in range(nx - 1)), g_xs[x])
    g_z = start_exchange("z", 0, g_zs, g_zrx, zs)

    for k in range(nz):
        cols = buf[:, :, cb * k: cb * (k + 1)].reshape(rows, cb)
        t_own[:, k] = dot(p_t[c], cols).reshape(t_shape)
    arrived(t_go)

    def add_core(i, carry):
        total = t_own[i] + t_core[i].astype(F32)
        t_own[i] = total
        t_xs[i] = total.astype(BF16)
        return carry

    lax.fori_loop(0, nx, add_core, 0)
    t_copies = {"x": start_scatter("x", 1, t_xs, t_xrx, xs)}

    arrived(g_z)
    g_all[c, x, y] = sum((g_zrx[d] for d in range(nz - 1)), g_zs[...])
    g_xy = []
    for n, d in enumerate(plane):
        go = copy(g_all.at[c, x, y], g_all.at[c, x, y], xy_s.at[n], xy_r.at[n], hop("xy", d))
        go.start()
        g_xy.append(go)
    for n, d in enumerate(plane):
        part = g_all.at[c, lax.rem(x - d[0] + nx, nx), lax.rem(y - d[1] + ny, ny)]
        copy(part, part, xy_s.at[n], xy_r.at[n], hop("xy", d)).wait_recv()
    pending += g_xy
    g_gc = copy(g_all.at[c], g_all.at[c], core_s.at[nx + 2], core_r.at[nx + 2], hop("core", 1))
    g_gc.start()
    copy(g_all.at[other], g_all.at[other], core_s.at[nx + 2], core_r.at[nx + 2], hop("core", 1)).wait_recv()
    pending += [g_gc]

    def sum_x():
        arrived(t_copies["x"])

        def add_x(k, carry):
            total = t_own[x, k]
            for d in range(nx - 1):
                total = total + t_xrx[d, k].astype(F32)
            t_own[x, k] = total
            t_zs[k] = total.astype(BF16)
            return carry

        lax.fori_loop(0, nz, add_x, 0)
        t_copies["z"] = start_scatter("z", 1, t_zs, t_zrx, zs)

    def sum_z():
        arrived(t_copies["z"])
        t_all[c, x, z] = sum((t_zrx[d].astype(F32) for d in range(nz - 1)), t_own[x, z]).astype(BF16)
        t_copies["gz"] = start_gather("z", 2, lambda i: t_all.at[c, x, i], zs)

    def gather_x():
        gathered("z", 2, lambda i: t_all.at[c, x, i], t_copies["gz"], zs)
        t_copies["gx"] = start_gather("x", 2, lambda i: t_all.at[c, i], xs)

    def gather_core():
        gathered("x", 2, lambda i: t_all.at[c, i], t_copies["gx"], xs)
        go = copy(t_all.at[c], t_all.at[c], core_s.at[nx + 1], core_r.at[nx + 1], hop("core", 1))
        go.start()
        copy(t_all.at[other], t_all.at[other], core_s.at[nx + 1], core_r.at[nx + 1], hop("core", 1)).wait_recv()
        pending.append(go)

    nb = rank // 128
    gr = g_all.shape[3] * g_all.shape[4]
    for i in range(2):
        for j in range(nx):
            for k in range(ny):
                lo = (i * nx + j) * gr
                m[lo:lo + gr, gcols * k:gcols * (k + 1)] = g_all[i, j, k].reshape(gr, gcols)
    row = lax.broadcasted_iota(jnp.int32, (128, 128), 0)
    col = lax.broadcasted_iota(jnp.int32, (128, 128), 1)
    eye = jnp.where(row == col, 1.0, 0.0)
    for i in range(nb):
        for j in range(nb):
            m[128 * i:128 * (i + 1), rank + 128 * j:rank + 128 * (j + 1)] = eye if i == j else jnp.zeros_like(eye)
    steps = 16 * nb
    plan = {2 * steps // 64: sum_x, 22 * steps // 64: sum_z, 42 * steps // 64: gather_x}
    for k in range(nb):
        lo, hi = 128 * k, 128 * (k + 1)
        w[:, 0:128] = m[lo:hi, lo:hi]
        w[:, 128:256] = eye
        factor128(w, {n - 16 * k: f for n, f in plan.items()})
        inv = w[:, 128:256]
        m[lo:hi, hi:rank + hi] = dot(inv, m[lo:hi, hi:rank + hi], precision=HIGHEST)
        if k + 1 < nb:
            m[hi:, hi:rank + hi] = m[hi:, hi:rank + hi] - dot(
                m[lo:hi, hi:rank], m[lo:hi, hi:rank + hi], ((0,), (0,)), HIGHEST)
    high, low = split(m[:, rank:])
    orth_ref[...] = (dot(p_all, high, ((1,), (1,))) + dot(p_all, low, ((1,), (1,)))).astype(BF16)
    gather_core()

    ones = jnp.ones((8, cb), F32)
    total = jnp.zeros((8, rank), F32)
    for k in range(nz):
        t = t_all[:, :, k].reshape(rank, cb)
        r = dot(high, t) + dot(low, t)
        r_ref[:, cb * k:cb * (k + 1)] = r.astype(BF16)
        nb_ref[:, cb * k:cb * (k + 1)] = r.astype(F32)
        total = total + dot(ones, r * r, ((1,), (1,)), HIGHEST)
    sq_own[...] = total
    sq_go = start_exchange("y", 2, sq_own, sq_rx, ys)
    arrived(sq_go)
    total = sum((sq_rx[d] for d in range(ny - 1)), sq_own[...])
    scale = lax.rsqrt(total / cols_total + 1e-06)
    scale = dot(scale, jnp.full((8, 128), 0.125, F32), ((0,), (0,)), HIGHEST)
    for k in range(nz * cb // 128):
        nb_ref[:, 128 * k:128 * (k + 1)] = nb_ref[:, 128 * k:128 * (k + 1)] * scale
    for go in pending:
        go.wait_send()


def update_call(shape, cols_total, mom, grad, basis):
    nx, nz, ny = shape
    rows, cols = mom.shape
    rank = basis.shape[1]
    part, cb, rb, gb = rows // ny, cols // nz, rank // (2 * nx), rank // (2 * nx * nz)
    gc = rank // ny
    vmem, sem = pltpu.VMEM, pltpu.SemaphoreType.DMA
    space = pl.BlockSpec(memory_space=pltpu.VMEM)
    hbm = pl.BlockSpec(memory_space=pl.ANY)
    return pl.pallas_call(
        functools.partial(update_kernel, shape, cols_total),
        out_shape=(
            jax.ShapeDtypeStruct((rows, rank), BF16),
            jax.ShapeDtypeStruct((rank, cols), BF16),
            jax.ShapeDtypeStruct((rank, cols), F32),
            jax.ShapeDtypeStruct((ny, part, cols), BF16),
        ),
        in_specs=[hbm] * 3,
        out_specs=(space,) * 4,
        scratch_shapes=[
            vmem((ny, part, cols), BF16),
            vmem((ny, part, cols), BF16),
            vmem((cols, rank), BF16),
            vmem((ny - 1, part, rank), BF16),
            vmem((ny - 1, part, rank), BF16),
            vmem((ny, part, rank), BF16),
            vmem((2, rank // 2, rows), BF16),
            vmem((nx, nz, gb, gc), F32),
            vmem((nx, nz, gb, gc), F32),
            vmem((nx, nz, gb, gc), F32),
            vmem((nx, nz, gb, gc), F32),
            vmem((nx - 1, nz, gb, gc), F32),
            vmem((nz, gb, gc), F32),
            vmem((nz - 1, nz, gb, gc), F32),
            vmem((2, nx, ny, nz, gb, gc), F32),
            vmem((nx, nz, rb, cb), BF16),
            vmem((nx, nz, rb, cb), F32),
            vmem((nx, nz, rb, cb), BF16),
            vmem((nx, nz, rb, cb), BF16),
            vmem((nx - 1, nz, rb, cb), BF16),
            vmem((nz, rb, cb), BF16),
            vmem((nz - 1, rb, cb), BF16),
            vmem((2, nx, nz, rb, cb), BF16),
            vmem((rank, 2 * rank), F32),
            vmem((128, 256), F32),
            vmem((8, rank), F32),
            vmem((ny - 1, 8, rank), F32),
            sem((3, ny)),
            sem((nx + 3,)), sem((nx + 3,)),
            sem((3, nx - 1)), sem((3, nx - 1)),
            sem((3, ny - 1)), sem((3, ny - 1)),
            sem((3, nz - 1)), sem((3, nz - 1)),
            sem((nx * ny - 1,)), sem((nx * ny - 1,)),
        ],
        compiler_params=pltpu.CompilerParams(
            collective_id=0, has_side_effects=True, vmem_limit_bytes=VMEM_LIMIT),
        name="update",
    )(mom.reshape(ny, part, cols), grad.reshape(ny, part, cols), basis)


def factor8(cols):
    e = [[jnp.broadcast_to(cols[k][q:q + 1, :], (8, 128)) for k in range(q + 1)] for q in range(8)]
    low = [[None] * 8 for _ in range(8)]
    inv = [[None] * 8 for _ in range(8)]
    for p in range(8):
        inv[p][p] = lax.rsqrt(e[p][p])
        for q in range(p + 1, 8):
            low[q][p] = e[q][p] * inv[p][p]
        for q in range(p + 1, 8):
            for k in range(p + 1, q + 1):
                e[q][k] = e[q][k] - low[q][p] * low[k][p]
    for q in range(8):
        for k in range(q):
            acc = low[q][k] * inv[k][k]
            for m in range(k + 1, q):
                acc = acc + low[q][m] * inv[m][k]
            inv[q][k] = -acc * inv[q][q]
    return inv


def lanes(x, k):
    return jnp.broadcast_to(x[:, k:k + 1], (8, 128))


def rows8(x, k):
    return jnp.broadcast_to(x[k:k + 1, :], (8, 128))


def factor128(r, between):
    sub = lax.broadcasted_iota(jnp.int32, (8, 128), 0)
    for s in range(16):
        if s in between:
            between[s]()
        lo = 8 * s
        a, v = r[lo:lo + 8, 0:128], r[lo:lo + 8, 128:256]
        cols = [lanes(a, lo + k) for k in range(8)]
        if s < 15:
            an, vn = r[lo + 8:lo + 16, 0:128], r[lo + 8:lo + 16, 128:256]
            nxt = [lanes(an, lo + k) for k in range(8)]
        inv = factor8(cols)
        new_a = new_v = None
        for k in range(8):
            m = jnp.where(sub == k, inv[k][k], 0.0)
            for q in range(k + 1, 8):
                m = jnp.where(sub == q, inv[q][k], m)
            ta, tv = m * rows8(a, k), m * rows8(v, k)
            new_a = ta if new_a is None else new_a + ta
            new_v = tv if new_v is None else new_v + tv
        r[lo:lo + 8, 128:256] = new_v
        if s < 15:
            for k in range(8):
                lc = nxt[0] * inv[k][0]
                for j in range(1, k + 1):
                    lc = lc + nxt[j] * inv[k][j]
                an = an - lc * rows8(new_a, k)
                vn = vn - lc * rows8(new_v, k)
            r[lo + 8:lo + 16, 0:128], r[lo + 8:lo + 16, 128:256] = an, vn
        if s < 14:
            both = jnp.concatenate([new_a, new_v], axis=1)
            update = dot(new_a, both, ((0,), (0,)), HIGHEST)
            r[lo + 16:128, :] = r[lo + 16:128, :] - update[lo + 16:128, :]


def split(x):
    high = x.astype(BF16)
    return high, (x - high.astype(F32)).astype(BF16)


def outputs_kernel(orth, buf, r_t, nb_t, mom_out, basis_out, dir_out):
    factor = orth[...]
    low_rank = dot(factor, r_t[...])
    mom_out[...] = (buf[...].astype(F32) - 0.05 * low_rank).astype(BF16)
    new_basis = nb_t[...].astype(BF16)
    dir_out[...] = (math.sqrt(ROWS / RANK) * dot(factor, new_basis)).astype(BF16)
    basis_out[...] = new_basis.T


def outputs_call(orth, buf, r_t, nb_t):
    rows, cols = buf.shape
    rank = orth.shape[1]
    wide = 256
    block = lambda shape, place: pl.BlockSpec(shape, place)
    return pl.pallas_call(
        outputs_kernel,
        grid=(cols // wide,),
        out_shape=(
            jax.ShapeDtypeStruct((rows, cols), BF16),
            jax.ShapeDtypeStruct((cols, rank), BF16),
            jax.ShapeDtypeStruct((rows, cols), BF16),
        ),
        in_specs=[
            block((rows, rank), lambda i: (0, 0)),
            block((rows, wide), lambda i: (0, i)),
            block((rank, wide), lambda i: (0, i)),
            block((rank, wide), lambda i: (0, i)),
        ],
        out_specs=(
            block((rows, wide), lambda i: (0, i)),
            block((wide, rank), lambda i: (i, 0)),
            block((rows, wide), lambda i: (0, i)),
        ),
        compiler_params=pltpu.CompilerParams(vmem_limit_bytes=VMEM_LIMIT),
        name="outputs",
    )(orth, buf, r_t, nb_t)


def per_device(momentum, gradient, old_basis):
    orth, r_t, nb_t, buf = update_call(SHAPE, COLS, momentum, gradient, old_basis)
    return outputs_call(orth, buf.reshape(momentum.shape), r_t, nb_t)


def solution(mesh):
    in_specs = (P("zero", "tensor"), P("zero", "tensor"), P("tensor", None))
    out_specs = (P("zero", "tensor"), P("tensor", None), P("zero", "tensor"))
    return jax.shard_map(
        per_device, mesh=mesh, in_specs=in_specs, out_specs=out_specs, check_vma=False
    )
```

time: 146 us -> 112 us (0.77); the launches traced: 144 us -> 112 us
  blocking collectives: 17.7 us -> 0 us
  matrix products: 7.3 us -> 0 us
  Pallas kernels: 115 us -> 111 us
  local copies, waits for them, and re-layouts: 2.53 us -> 0 us
    psum x1 -> x0, blocking collectives: 17.7 us -> none  [per_device(): col_squares = lax.psum(squares, 'tensor')]
    dot_general x2 -> x0, matrix products: 7.3 us -> none  [dot(): lax.dot_general(a, b, (contract, ((), ())), precision=precision, preferre...]
    pallas_call x2, Pallas kernels: 115 us -> 111 us  [the longest x1 102 us: update_call(): pl.pallas_call(functools.partial(update_kernel, shape, cols_total), out_s...]
    unnamed x9 -> x0, local copies, waits for them, and re-layouts: 2.53 us -> none
where the time goes in v2:
time: 112 us
  Pallas kernels  111 us (99%)
    pallas_call x1, Pallas kernels, update_call(): pl.pallas_call(functools.partial(update_kernel, shape, cols_total), out_s...  102 us
    pallas_call x1, Pallas kernels, outputs_call(): pl.pallas_call(outputs_kernel, grid=(cols // wide,), out_shape=(jax.Shape...  9.39 us

profile of v2, /device:TPU:1, one launch (start us, length us, event | category | flops | bytes accessed | tf_op | source)
XLA Modules:
  0.0 111.8 jit_solution(5568498823988333496)
XLA Ops:
  0.6 101.8 %update.1 = (bf16[448,512]{1,0:T(8,128)(2,1)}, bf16[512,2048]{1,0:T(8,128)(2,1)}, f32[512,2048]{1,0:T(8,128)}, bf16[4,112,2048]{2,1,0:T(8,128)(2,1)}) custom-call(bf16[4,112,2048]{2,1,0:T(8,128)(2,1)} %bitcast.3, bf16[4,112,2048]{2,1,0:T(8,128)(2,1)} %bitcast.4, bf16[2048,512]{1,0:T(8,128)(2,1)} %basis_hbm.1), custom_call_target="tpu_custom_call" | custom-call | tf_op jit(solution)/shard_map/update/pallas_call | solution.py:302
  102.4 9.4 %outputs.1 = (bf16[448,2048]{1,0:T(8,128)(2,1)}, bf16[2048,512]{1,0:T(8,128)(2,1)}, bf16[448,2048]{1,0:T(8,128)(2,1)}) custom-call(bf16[448,512]{1,0:T(8,128)(2,1)} %get-tuple-element.7.orth, bf16[448,2048]{1,0:T(8,128)(2,1)} %bitcast.5, bf16[512,2048]{1,0:T(8,128)(2,1)} %get-tuple-element.9.r_t, f32[512,2048]{1,0:T(8,128)} %get-tuple-element.10.nb_t), custom_call_target="tpu_custom_call" | custom-call | tf_op jit(solution)/shard_map/outputs/pallas_call | solution.py:435

commit v3 on v2

--- a/solution.py
+++ b/solution.py
@@ -15,7 +15,8 @@
 BF16 = jnp.bfloat16
 HIGHEST = lax.Precision.HIGHEST
 SHAPE = (4, 8, 4)
-VMEM_LIMIT = 56 * 1024 * 1024
+VMEM_LIMIT = 40 * 1024 * 1024
+PIECES = 4
 
 
 def dot(a, b, contract=((1,), (0,)), precision=None):
@@ -27,8 +28,8 @@
 def update_kernel(shape, cols_total, mom_hbm, grad_hbm, basis_hbm, orth_ref, r_ref, nb_ref, buf,
                   mom, grad, basis, p_part, p_rx, p_sum, p_t,
                   g_send, g_own, g_core, g_xs, g_xrx, g_zs, g_zrx, g_all,
-                  t_send, t_own, t_core, t_xs, t_xrx, t_zs, t_zrx, t_all,
-                  m, w, sq_own, sq_rx, in_s, core_s, core_r, x_s, x_r, y_s, y_r, z_s, z_r, xy_s, xy_r):
+                  t_send, t_own, t_core, t_xs, t_xrx, t_zf, t_zs, t_zrx, t_all,
+                  r_f32, m, w, sq_own, sq_rx, in_s, core_s, core_r, x_s, x_r, y_s, y_r, z_s, z_r, xy_s, xy_r):
     nx, nz, ny = shape
     zero, y = lax.axis_index("zero"), lax.axis_index("tensor")
     c = lax.rem(zero, 2)
@@ -135,21 +136,29 @@
     for d in y_order[:-1]:
         p_part[d - 1] = partial_rows(d).astype(BF16)
     pl.semaphore_wait(barrier, len(peers))
+    rank = p_sum.shape[2]
+    sides = [pl.ds(0, rank // 2), pl.ds(rank // 2, rank // 2)]
     p_go = []
-    for d in y_order[:-1]:
-        go = copy(p_part.at[d - 1], p_rx.at[d - 1], y_s.at[0, d - 1], y_r.at[0, d - 1], hop("y", d))
-        go.start()
-        p_go.append(go)
+    for n, side in enumerate(sides):
+        p_go.append([])
+        for d in y_order[:-1]:
+            go = copy(p_part.at[d - 1, :, side], p_rx.at[d - 1, :, side],
+                      y_s.at[n, d - 1], y_r.at[n, d - 1], hop("y", d))
+            go.start()
+            p_go[n].append(go)
     own = partial_rows(0)
-    for d, go in zip(y_order, p_go):
-        go.wait_recv()
-        own = own + p_rx[d - 1].astype(F32)
-    p_sum[y] = own.astype(BF16)
-    pending += p_go
-    p_go = start_gather("y", 1, lambda i: p_sum.at[i], ys)
-    gathered("y", 1, lambda i: p_sum.at[i], p_go, ys)
-
-    rows, rank = buf.shape[0] * buf.shape[1], p_sum.shape[2]
+    p_gather = []
+    for n, side in enumerate(sides):
+        arrived(p_go[n])
+        total = own[:, n * rank // 2:(n + 1) * rank // 2]
+        for d in y_order[:-1]:
+            total = total + p_rx[d - 1, :, side].astype(F32)
+        p_sum[y, :, side] = total.astype(BF16)
+        p_gather.append(start_gather("y", 2 + n, lambda i: p_sum.at[i, :, side], ys))
+    for n, side in enumerate(sides):
+        gathered("y", 2 + n, lambda i: p_sum.at[i, :, side], p_gather[n], ys)
+
+    rows = buf.shape[0] * buf.shape[1]
     half = rank // 2
     p_all = p_sum[...].reshape(rows, rank)
     p_t[...] = p_all.T.reshape(2, half, rows)
@@ -167,33 +176,68 @@
     g_xs[...] = g_own[...] + g_core[...]
     g_x = start_scatter("x", 0, g_xs, g_xrx, xs)
 
-    cb = t_send.shape[3]
-    t_shape = (t_send.shape[0], t_send.shape[2], cb)
+    pieces, _, _, tr, cb = t_send.shape
+    t_shape = (pieces, nx, tr, cb)
     for k in range(nz):
         cols = buf[:, :, cb * k: cb * (k + 1)].reshape(rows, cb)
-        t_send[:, k] = dot(p_t[other], cols).astype(BF16).reshape(t_shape)
-    t_go = []
-    for i in range(nx):
-        go = copy(t_send.at[i], t_core.at[i], core_s.at[1 + i], core_r.at[1 + i], hop("core", 1))
+        t_send[:, :, k] = dot(p_t[other], cols).astype(BF16).reshape(t_shape)
+    t_core_go = []
+    for p in range(pieces):
+        go = copy(t_send.at[p], t_core.at[p], core_s.at[2 + p], core_r.at[2 + p], hop("core", 1))
         go.start()
-        t_go.append(go)
+        t_core_go.append(go)
+    for k in range(nz):
+        cols = buf[:, :, cb * k: cb * (k + 1)].reshape(rows, cb)
+        t_own[:, :, k] = dot(p_t[c], cols).reshape(t_shape)
+
+    t_go = {}
+
+    def sum_core(p):
+        arrived([t_core_go[p]])
+        total = t_own[p] + t_core[p].astype(F32)
+        t_own[p] = total
+        t_xs[p] = total.astype(BF16)
+        t_go["x", p] = start_scatter("x", 1 + p, t_xs.at[p], t_xrx.at[p], xs)
+
+    def sum_x(p):
+        arrived(t_go["x", p])
+        total = t_own[p, x]
+        for d in range(nx - 1):
+            total = total + t_xrx[p, d].astype(F32)
+        t_zf[p] = total
+        t_zs[p] = total.astype(BF16)
+        t_go["z", p] = start_scatter("z", 1 + p, t_zs.at[p], t_zrx.at[p], zs)
+
+    def sum_z(p):
+        arrived(t_go["z", p])
+        total = t_zf[p, z]
+        for d in range(nz - 1):
+            total = total + t_zrx[p, d].astype(F32)
+        t_all[c, p, x, z] = total.astype(BF16)
+        t_go["gz", p] = start_gather("z", 1 + pieces + p, lambda i: t_all.at[c, p, x, i], zs)
+
+    def gather_x(p):
+        gathered("z", 1 + pieces + p, lambda i: t_all.at[c, p, x, i], t_go["gz", p], zs)
+        t_go["gx", p] = start_gather("x", 1 + pieces + p, lambda i: t_all.at[c, p, i], xs)
+
+    def gather_core(p):
+        gathered("x", 1 + pieces + p, lambda i: t_all.at[c, p, i], t_go["gx", p], xs)
+        t_go["gc", p] = copy(t_all.at[c, p], t_all.at[c, p], core_s.at[2 + pieces + p],
+                             core_r.at[2 + pieces + p], hop("core", 1))
+        t_go["gc", p].start()
+
+    def got_core(p):
+        part = t_all.at[other, p]
+        copy(part, part, core_s.at[2 + pieces + p], core_r.at[2 + pieces + p], hop("core", 1)).wait_recv()
+        pending.append(t_go["gc", p])
+
     arrived(g_x)
     g_zs[...] = sum((g_xrx[d] for d in range(nx - 1)), g_xs[x])
     g_z = start_exchange("z", 0, g_zs, g_zrx, zs)
-
-    for k in range(nz):
-        cols = buf[:, :, cb * k: cb * (k + 1)].reshape(rows, cb)
-        t_own[:, k] = dot(p_t[c], cols).reshape(t_shape)
-    arrived(t_go)
-
-    def add_core(i, carry):
-        total = t_own[i] + t_core[i].astype(F32)
-        t_own[i] = total
-        t_xs[i] = total.astype(BF16)
-        return carry
-
-    lax.fori_loop(0, nx, add_core, 0)
-    t_copies = {"x": start_scatter("x", 1, t_xs, t_xrx, xs)}
+    for p in range(pieces):
+        sum_core(p)
+    for p in range(pieces // 2):
+        sum_x(p)
 
     arrived(g_z)
     g_all[c, x, y] = sum((g_zrx[d] for d in range(nz - 1)), g_zs[...])
@@ -202,44 +246,20 @@
         go = copy(g_all.at[c, x, y], g_all.at[c, x, y], xy_s.at[n], xy_r.at[n], hop("xy", d))
         go.start()
         g_xy.append(go)
+    for p in range(pieces // 2, pieces):
+        sum_x(p)
+    for p in range(pieces // 2):
+        sum_z(p)
     for n, d in enumerate(plane):
         part = g_all.at[c, lax.rem(x - d[0] + nx, nx), lax.rem(y - d[1] + ny, ny)]
         copy(part, part, xy_s.at[n], xy_r.at[n], hop("xy", d)).wait_recv()
     pending += g_xy
-    g_gc = copy(g_all.at[c], g_all.at[c], core_s.at[nx + 2], core_r.at[nx + 2], hop("core", 1))
+    g_gc = copy(g_all.at[c], g_all.at[c], core_s.at[1], core_r.at[1], hop("core", 1))
     g_gc.start()
-    copy(g_all.at[other], g_all.at[other], core_s.at[nx + 2], core_r.at[nx + 2], hop("core", 1)).wait_recv()
+    for p in range(pieces // 2, pieces):
+        sum_z(p)
+    copy(g_all.at[other], g_all.at[other], core_s.at[1], core_r.at[1], hop("core", 1)).wait_recv()
     pending += [g_gc]
-
-    def sum_x():
-        arrived(t_copies["x"])
-
-        def add_x(k, carry):
-            total = t_own[x, k]
-            for d in range(nx - 1):
-                total = total + t_xrx[d, k].astype(F32)
-            t_own[x, k] = total
-            t_zs[k] = total.astype(BF16)
-            return carry
-
-        lax.fori_loop(0, nz, add_x, 0)
-        t_copies["z"] = start_scatter("z", 1, t_zs, t_zrx, zs)
-
-    def sum_z():
-        arrived(t_copies["z"])
-        t_all[c, x, z] = sum((t_zrx[d].astype(F32) for d in range(nz - 1)), t_own[x, z]).astype(BF16)
-        t_copies["gz"] = start_gather("z", 2, lambda i: t_all.at[c, x, i], zs)
-
-    def gather_x():
-        gathered("z", 2, lambda i: t_all.at[c, x, i], t_copies["gz"], zs)
-        t_copies["gx"] = start_gather("x", 2, lambda i: t_all.at[c, i], xs)
-
-    def gather_core():
-        gathered("x", 2, lambda i: t_all.at[c, i], t_copies["gx"], xs)
-        go = copy(t_all.at[c], t_all.at[c], core_s.at[nx + 1], core_r.at[nx + 1], hop("core", 1))
-        go.start()
-        copy(t_all.at[other], t_all.at[other], core_s.at[nx + 1], core_r.at[nx + 1], hop("core", 1)).wait_recv()
-        pending.append(go)
 
     nb = rank // 128
     gr = g_all.shape[3] * g_all.shape[4]
@@ -254,8 +274,10 @@
     for i in range(nb):
         for j in range(nb):
             m[128 * i:128 * (i + 1), rank + 128 * j:rank + 128 * (j + 1)] = eye if i == j else jnp.zeros_like(eye)
-    steps = 16 * nb
-    plan = {2 * steps // 64: sum_x, 22 * steps // 64: sum_z, 42 * steps // 64: gather_x}
+    stages = [(gather_x, p) for p in range(pieces)] + [(gather_core, p) for p in range(pieces)]
+    first = (2, 4, 12, 20, 36, 44, 52, 60)
+    plan = {at_step * nb // 4: stage for at_step, stage in zip(first, stages)}
+    assert len(plan) == len(stages)
     for k in range(nb):
         lo, hi = 128 * k, 128 * (k + 1)
         w[:, 0:128] = m[lo:hi, lo:hi]
@@ -268,24 +290,26 @@
                 m[lo:hi, hi:rank], m[lo:hi, hi:rank + hi], ((0,), (0,)), HIGHEST)
     high, low = split(m[:, rank:])
     orth_ref[...] = (dot(p_all, high, ((1,), (1,))) + dot(p_all, low, ((1,), (1,)))).astype(BF16)
-    gather_core()
+    for p in range(pieces):
+        got_core(p)
 
     ones = jnp.ones((8, cb), F32)
     total = jnp.zeros((8, rank), F32)
     for k in range(nz):
-        t = t_all[:, :, k].reshape(rank, cb)
+        t = t_all[:, :, :, k].reshape(rank, cb)
         r = dot(high, t) + dot(low, t)
         r_ref[:, cb * k:cb * (k + 1)] = r.astype(BF16)
-        nb_ref[:, cb * k:cb * (k + 1)] = r.astype(F32)
+        r_f32[:, cb * k:cb * (k + 1)] = r
         total = total + dot(ones, r * r, ((1,), (1,)), HIGHEST)
     sq_own[...] = total
-    sq_go = start_exchange("y", 2, sq_own, sq_rx, ys)
+    sq_go = start_exchange("y", 4, sq_own, sq_rx, ys)
     arrived(sq_go)
     total = sum((sq_rx[d] for d in range(ny - 1)), sq_own[...])
     scale = lax.rsqrt(total / cols_total + 1e-06)
     scale = dot(scale, jnp.full((8, 128), 0.125, F32), ((0,), (0,)), HIGHEST)
     for k in range(nz * cb // 128):
-        nb_ref[:, 128 * k:128 * (k + 1)] = nb_ref[:, 128 * k:128 * (k + 1)] * scale
+        part = pl.ds(128 * k, 128)
+        nb_ref[:, part] = (r_f32[:, part] * scale).astype(BF16)
     for go in pending:
         go.wait_send()
 
@@ -294,18 +318,20 @@
     nx, nz, ny = shape
     rows, cols = mom.shape
     rank = basis.shape[1]
-    part, cb, rb, gb = rows // ny, cols // nz, rank // (2 * nx), rank // (2 * nx * nz)
-    gc = rank // ny
+    part, cb, gb = rows // ny, cols // nz, rank // (2 * nx * nz)
+    gc, np = rank // ny, PIECES
+    tr = rank // (2 * np * nx)
+    args = (mom.reshape(ny, part, cols), grad.reshape(ny, part, cols), basis)
     vmem, sem = pltpu.VMEM, pltpu.SemaphoreType.DMA
     space = pl.BlockSpec(memory_space=pltpu.VMEM)
-    hbm = pl.BlockSpec(memory_space=pl.ANY)
+    hbm = pl.BlockSpec(memory_space=pltpu.MemorySpace.HBM)
     return pl.pallas_call(
         functools.partial(update_kernel, shape, cols_total),
         out_shape=(
-            jax.ShapeDtypeStruct((rows, rank), BF16),
-            jax.ShapeDtypeStruct((rank, cols), BF16),
-            jax.ShapeDtypeStruct((rank, cols), F32),
-            jax.ShapeDtypeStruct((ny, part, cols), BF16),
+            vmem((rows, rank), BF16),
+            vmem((rank, cols), BF16),
+            vmem((rank, cols), BF16),
+            vmem((ny, part, cols), BF16),
         ),
         in_specs=[hbm] * 3,
         out_specs=(space,) * 4,
@@ -325,29 +351,31 @@
             vmem((nz, gb, gc), F32),
             vmem((nz - 1, nz, gb, gc), F32),
             vmem((2, nx, ny, nz, gb, gc), F32),
-            vmem((nx, nz, rb, cb), BF16),
-            vmem((nx, nz, rb, cb), F32),
-            vmem((nx, nz, rb, cb), BF16),
-            vmem((nx, nz, rb, cb), BF16),
-            vmem((nx - 1, nz, rb, cb), BF16),
-            vmem((nz, rb, cb), BF16),
-            vmem((nz - 1, rb, cb), BF16),
-            vmem((2, nx, nz, rb, cb), BF16),
+            vmem((np, nx, nz, tr, cb), BF16),
+            vmem((np, nx, nz, tr, cb), F32),
+            vmem((np, nx, nz, tr, cb), BF16),
+            vmem((np, nx, nz, tr, cb), BF16),
+            vmem((np, nx - 1, nz, tr, cb), BF16),
+            vmem((np, nz, tr, cb), F32),
+            vmem((np, nz, tr, cb), BF16),
+            vmem((np, nz - 1, tr, cb), BF16),
+            vmem((2, np, nx, nz, tr, cb), BF16),
+            vmem((rank, cols), F32),
             vmem((rank, 2 * rank), F32),
             vmem((128, 256), F32),
             vmem((8, rank), F32),
             vmem((ny - 1, 8, rank), F32),
             sem((3, ny)),
-            sem((nx + 3,)), sem((nx + 3,)),
-            sem((3, nx - 1)), sem((3, nx - 1)),
-            sem((3, ny - 1)), sem((3, ny - 1)),
-            sem((3, nz - 1)), sem((3, nz - 1)),
+            sem((2 + 2 * np,)), sem((2 + 2 * np,)),
+            sem((1 + 2 * np, nx - 1)), sem((1 + 2 * np, nx - 1)),
+            sem((5, ny - 1)), sem((5, ny - 1)),
+            sem((1 + 2 * np, nz - 1)), sem((1 + 2 * np, nz - 1)),
             sem((nx * ny - 1,)), sem((nx * ny - 1,)),
         ],
         compiler_params=pltpu.CompilerParams(
             collective_id=0, has_side_effects=True, vmem_limit_bytes=VMEM_LIMIT),
         name="update",
-    )(mom.reshape(ny, part, cols), grad.reshape(ny, part, cols), basis)
+    )(*(pltpu.with_memory_space_constraint(v, pltpu.MemorySpace.HBM) for v in args))
 
 
 def factor8(cols):
@@ -378,17 +406,34 @@
     return jnp.broadcast_to(x[k:k + 1, :], (8, 128))
 
 
+def split3(x):
+    high = x.astype(BF16).astype(F32)
+    x = x - high
+    mid = x.astype(BF16).astype(F32)
+    return high, mid, x - mid
+
+
+def rank8(a, v):
+    ha, ma, la = split3(a)
+    hv, mv, lv = split3(v)
+    left = jnp.concatenate([ha, ma, la, ha, ma, ha], axis=0).astype(BF16)
+    right_a = jnp.concatenate([ha, ha, ha, ma, ma, la], axis=0)
+    right_v = jnp.concatenate([hv, hv, hv, mv, mv, lv], axis=0)
+    return dot(left, jnp.concatenate([right_a, right_v], axis=1).astype(BF16), ((0,), (0,)))
+
+
 def factor128(r, between):
     sub = lax.broadcasted_iota(jnp.int32, (8, 128), 0)
+    a, v = r[0:8, 0:128], r[0:8, 128:256]
+    cols = [lanes(a, k) for k in range(8)]
     for s in range(16):
         if s in between:
-            between[s]()
+            between[s][0](between[s][1])
         lo = 8 * s
-        a, v = r[lo:lo + 8, 0:128], r[lo:lo + 8, 128:256]
-        cols = [lanes(a, lo + k) for k in range(8)]
         if s < 15:
             an, vn = r[lo + 8:lo + 16, 0:128], r[lo + 8:lo + 16, 128:256]
-            nxt = [lanes(an, lo + k) for k in range(8)]
+            below = [lanes(an, lo + k) for k in range(8)]
+            ahead = [lanes(an, lo + 8 + k) for k in range(8)]
         inv = factor8(cols)
         new_a = new_v = None
         for k in range(8):
@@ -400,17 +445,23 @@
             new_v = tv if new_v is None else new_v + tv
         r[lo:lo + 8, 128:256] = new_v
         if s < 15:
+            low = []
             for k in range(8):
-                lc = nxt[0] * inv[k][0]
+                acc = below[0] * inv[k][0]
                 for j in range(1, k + 1):
-                    lc = lc + nxt[j] * inv[k][j]
-                an = an - lc * rows8(new_a, k)
-                vn = vn - lc * rows8(new_v, k)
-            r[lo + 8:lo + 16, 0:128], r[lo + 8:lo + 16, 128:256] = an, vn
+                    acc = acc + below[j] * inv[k][j]
+                low.append(acc)
+            cols = []
+            for k in range(8):
+                an = an - low[k] * rows8(new_a, k)
+                vn = vn - low[k] * rows8(new_v, k)
+                acc = ahead[k]
+                for j in range(8):
+                    acc = acc - low[j] * rows8(low[j], k)
+                cols.append(acc)
+            a, v = an, vn
         if s < 14:
-            both = jnp.concatenate([new_a, new_v], axis=1)
-            update = dot(new_a, both, ((0,), (0,)), HIGHEST)
-            r[lo + 16:128, :] = r[lo + 16:128, :] - update[lo + 16:128, :]
+            r[lo + 16:128, :] = r[lo + 16:128, :] - rank8(new_a, new_v)[lo + 16:128, :]
 
 
 def split(x):
@@ -418,47 +469,61 @@
     return high, (x - high.astype(F32)).astype(BF16)
 
 
-def outputs_kernel(orth, buf, r_t, nb_t, mom_out, basis_out, dir_out):
+def outputs_kernel(orth, buf, r_t, nb_t, mom_hbm, basis_hbm, dir_hbm, mom_out, basis_out, dir_out, sems):
+    blocks, rows, wide = mom_out.shape
     factor = orth[...]
-    low_rank = dot(factor, r_t[...])
-    mom_out[...] = (buf[...].astype(F32) - 0.05 * low_rank).astype(BF16)
-    new_basis = nb_t[...].astype(BF16)
-    dir_out[...] = (math.sqrt(ROWS / RANK) * dot(factor, new_basis)).astype(BF16)
-    basis_out[...] = new_basis.T
+    copies = []
+    for i in range(blocks):
+        place = pl.ds(i * wide, wide)
+        low_rank = dot(factor, r_t[:, place])
+        mine = buf[:, :, place].reshape(rows, wide)
+        mom_out[i] = (mine.astype(F32) - 0.05 * low_rank).astype(BF16)
+        new_basis = nb_t[:, place]
+        basis_out[place, :] = new_basis.T
+        dir_out[i] = (math.sqrt(ROWS / RANK) * dot(factor, new_basis)).astype(BF16)
+        for n, (src, dst) in enumerate((
+            (mom_out.at[i], mom_hbm.at[:, place]),
+            (basis_out.at[place, :], basis_hbm.at[place, :]),
+            (dir_out.at[i], dir_hbm.at[:, place]),
+        )):
+            go = pltpu.make_async_copy(src, dst, sems.at[n, i])
+            go.start()
+            copies.append(go)
+    for go in copies:
+        go.wait()
 
 
 def outputs_call(orth, buf, r_t, nb_t):
-    rows, cols = buf.shape
+    rows, cols = buf.shape[0] * buf.shape[1], buf.shape[2]
     rank = orth.shape[1]
     wide = 256
-    block = lambda shape, place: pl.BlockSpec(shape, place)
+    blocks = cols // wide
+    space = pl.BlockSpec(memory_space=pltpu.VMEM)
+    hbm = pl.BlockSpec(memory_space=pl.ANY)
+    args = [pltpu.with_memory_space_constraint(v, pltpu.VMEM) for v in (orth, buf, r_t, nb_t)]
     return pl.pallas_call(
         outputs_kernel,
-        grid=(cols // wide,),
         out_shape=(
             jax.ShapeDtypeStruct((rows, cols), BF16),
             jax.ShapeDtypeStruct((cols, rank), BF16),
             jax.ShapeDtypeStruct((rows, cols), BF16),
         ),
-        in_specs=[
-            block((rows, rank), lambda i: (0, 0)),
-            block((rows, wide), lambda i: (0, i)),
-            block((rank, wide), lambda i: (0, i)),
-            block((rank, wide), lambda i: (0, i)),
+        in_specs=[space] * 4,
+        out_specs=(hbm,) * 3,
+        scratch_shapes=[
+            pltpu.VMEM((blocks, rows, wide), BF16),
+            pltpu.VMEM((cols, rank), BF16),
+            pltpu.VMEM((blocks, rows, wide), BF16),
+            pltpu.SemaphoreType.DMA((3, blocks)),
         ],
-        out_specs=(
-            block((rows, wide), lambda i: (0, i)),
-            block((wide, rank), lambda i: (i, 0)),
-            block((rows, wide), lambda i: (0, i)),
-        ),
         compiler_params=pltpu.CompilerParams(vmem_limit_bytes=VMEM_LIMIT),
         name="outputs",
-    )(orth, buf, r_t, nb_t)
+    )(*args)
 
 
 def per_device(momentum, gradient, old_basis):
     orth, r_t, nb_t, buf = update_call(SHAPE, COLS, momentum, gradient, old_basis)
-    return outputs_call(orth, buf.reshape(momentum.shape), r_t, nb_t)
+    return outputs_call(orth, buf, r_t, nb_t)
 
 
 def solution(mesh):

time: 112 us -> 86.5 us (0.77)
  Pallas kernels: 111 us -> 85.6 us
    pallas_call x1, Pallas kernels: 102 us -> 82.5 us  [update_call(): pl.pallas_call(functools.partial(update_kernel, shape, cols_total), out_s...]
    pallas_call x1, Pallas kernels: 9.39 us -> 3.15 us  [outputs_call(): pl.pallas_call(outputs_kernel, out_shape=(jax.ShapeDtypeStruct((rows, col...]
where the time goes in v3:
time: 86.5 us; the launch traced here: 86.4 us
  Pallas kernels  85.6 us (99%)
    pallas_call x1, Pallas kernels, update_call(): pl.pallas_call(functools.partial(update_kernel, shape, cols_total), out_s...  82.5 us
    pallas_call x1, Pallas kernels, outputs_call(): pl.pallas_call(outputs_kernel, out_shape=(jax.ShapeDtypeStruct((rows, col...  3.15 us

profile of v3, /device:TPU:1, one launch (start us, length us, event | category | flops | bytes accessed | tf_op | source)
XLA Modules:
  0.0 86.4 jit_solution(7854451822638786803)
XLA Ops:
  0.6 82.5 %update.1 = (bf16[448,512]{1,0:T(8,128)(2,1)S(1)}, bf16[512,2048]{1,0:T(8,128)(2,1)S(1)}, bf16[512,2048]{1,0:T(8,128)(2,1)S(1)}, bf16[4,112,2048]{2,1,0:T(8,128)(2,1)S(1)}) custom-call(bf16[4,112,2048]{2,1,0:T(8,128)(2,1)} %bitcast.2, bf16[4,112,2048]{2,1,0:T(8,128)(2,1)} %bitcast.3, bf16[2048,512]{1,0:T(8,128)(2,1)} %basis_hbm.1), custom_call_target="tpu_custom_call" | custom-call | tf_op jit(solution)/shard_map/update/pallas_call | solution.py:328
  83.1 3.1 %outputs.1 = (bf16[448,2048]{1,0:T(8,128)(2,1)}, bf16[2048,512]{1,0:T(8,128)(2,1)}, bf16[448,2048]{1,0:T(8,128)(2,1)}) custom-call(bf16[448,512]{1,0:T(8,128)(2,1)S(1)} %get-tuple-element.7.orth, bf16[4,112,2048]{2,1,0:T(8,128)(2,1)S(1)} %get-tuple-element.8.buf, bf16[512,2048]{1,0:T(8,128)(2,1)S(1)} %get-tuple-element.9.r_t, ...), custom_call_target="tpu_custom_call" | custom-call | tf_op jit(solution)/shard_map/outputs/pallas_call | solution.py:504

commit v4 on v3

--- a/solution.py
+++ b/solution.py
@@ -25,8 +25,8 @@
     )
 
 
-def update_kernel(shape, cols_total, mom_hbm, grad_hbm, basis_hbm, orth_ref, r_ref, nb_ref, buf,
-                  mom, grad, basis, p_part, p_rx, p_sum, p_t,
+def update_kernel(shape, cols_total, mom_hbm, grad_hbm, basis_hbm, orth_ref, mom_ref, nb_ref,
+                  buf, mom, grad, basis, p_part, p_rx, p_sum, p_t,
                   g_send, g_own, g_core, g_xs, g_xrx, g_zs, g_zrx, g_all,
                   t_send, t_own, t_core, t_xs, t_xrx, t_zf, t_zs, t_zrx, t_all,
                   r_f32, m, w, sq_own, sq_rx, in_s, core_s, core_r, x_s, x_r, y_s, y_r, z_s, z_r, xy_s, xy_r):
@@ -171,10 +171,6 @@
     g_send[...] = dot(p_t[other], p_mine).reshape(g_send.shape)
     g_go = copy(g_send, g_core, core_s.at[0], core_r.at[0], hop("core", 1))
     g_go.start()
-    g_own[...] = dot(p_t[c], p_mine).reshape(g_own.shape)
-    arrived([g_go])
-    g_xs[...] = g_own[...] + g_core[...]
-    g_x = start_scatter("x", 0, g_xs, g_xrx, xs)
 
     pieces, _, _, tr, cb = t_send.shape
     t_shape = (pieces, nx, tr, cb)
@@ -186,6 +182,11 @@
         go = copy(t_send.at[p], t_core.at[p], core_s.at[2 + p], core_r.at[2 + p], hop("core", 1))
         go.start()
         t_core_go.append(go)
+    g_own[...] = dot(p_t[c], p_mine).reshape(g_own.shape)
+    arrived([g_go])
+    g_xs[...] = g_own[...] + g_core[...]
+    g_x = start_scatter("x", 0, g_xs, g_xrx, xs)
+
     for k in range(nz):
         cols = buf[:, :, cb * k: cb * (k + 1)].reshape(rows, cb)
         t_own[:, :, k] = dot(p_t[c], cols).reshape(t_shape)
@@ -206,7 +207,7 @@
             total = total + t_xrx[p, d].astype(F32)
         t_zf[p] = total
         t_zs[p] = total.astype(BF16)
-        t_go["z", p] = start_scatter("z", 1 + p, t_zs.at[p], t_zrx.at[p], zs)
+        t_go["z", p] = start_scatter("z", 2 + p, t_zs.at[p], t_zrx.at[p], zs)
 
     def sum_z(p):
         arrived(t_go["z", p])
@@ -214,10 +215,10 @@
         for d in range(nz - 1):
             total = total + t_zrx[p, d].astype(F32)
         t_all[c, p, x, z] = total.astype(BF16)
-        t_go["gz", p] = start_gather("z", 1 + pieces + p, lambda i: t_all.at[c, p, x, i], zs)
+        t_go["gz", p] = start_gather("z", 2 + pieces + p, lambda i: t_all.at[c, p, x, i], zs)
 
     def gather_x(p):
-        gathered("z", 1 + pieces + p, lambda i: t_all.at[c, p, x, i], t_go["gz", p], zs)
+        gathered("z", 2 + pieces + p, lambda i: t_all.at[c, p, x, i], t_go["gz", p], zs)
         t_go["gx", p] = start_gather("x", 1 + pieces + p, lambda i: t_all.at[c, p, i], xs)
 
     def gather_core(p):
@@ -231,53 +232,66 @@
         copy(part, part, core_s.at[2 + pieces + p], core_r.at[2 + pieces + p], hop("core", 1)).wait_recv()
         pending.append(t_go["gc", p])
 
+    for p in range(pieces):
+        sum_core(p)
     arrived(g_x)
     g_zs[...] = sum((g_xrx[d] for d in range(nx - 1)), g_xs[x])
-    g_z = start_exchange("z", 0, g_zs, g_zrx, zs)
-    for p in range(pieces):
-        sum_core(p)
-    for p in range(pieces // 2):
-        sum_x(p)
-
-    arrived(g_z)
-    g_all[c, x, y] = sum((g_zrx[d] for d in range(nz - 1)), g_zs[...])
+    parts = [pl.ds(0, nz // 2), pl.ds(nz // 2, nz // 2)]
+    g_z = [start_exchange("z", n, g_zs.at[part], g_zrx.at[:, part], zs) for n, part in enumerate(parts)]
+
+    nb = rank // 128
+    row = lax.broadcasted_iota(jnp.int32, (128, 128), 0)
+    col = lax.broadcasted_iota(jnp.int32, (128, 128), 1)
+    eye = jnp.where(row == col, 1.0, 0.0)
+    for i in range(nb):
+        for j in range(nb):
+            m[128 * i:128 * (i + 1), rank + 128 * j:rank + 128 * (j + 1)] = eye if i == j else jnp.zeros_like(eye)
+
     g_xy = []
-    for n, d in enumerate(plane):
-        go = copy(g_all.at[c, x, y], g_all.at[c, x, y], xy_s.at[n], xy_r.at[n], hop("xy", d))
+    for h, part in enumerate(parts):
+        sum_x(h)
+        arrived(g_z[h])
+        g_all[c, x, y, part] = sum((g_zrx[d, part] for d in range(nz - 1)), g_zs[part])
+        for n, d in enumerate(plane):
+            mine = g_all.at[c, x, y, part]
+            go = copy(mine, mine, xy_s.at[h, n], xy_r.at[h, n], hop("xy", d))
+            go.start()
+            g_xy.append(go)
+    sum_x(2)
+    sum_z(0)
+    sum_x(3)
+    sum_z(1)
+    gather_x(0)
+    sum_z(2)
+    g_core_go = []
+    for h, part in enumerate(parts):
+        for n, d in enumerate(plane):
+            theirs = g_all.at[c, lax.rem(x - d[0] + nx, nx), lax.rem(y - d[1] + ny, ny), part]
+            copy(theirs, theirs, xy_s.at[h, n], xy_r.at[h, n], hop("xy", d)).wait_recv()
+        half_sem = [1, 2 + 2 * pieces][h]
+        mine = g_all.at[c, :, :, part]
+        go = copy(mine, mine, core_s.at[half_sem], core_r.at[half_sem], hop("core", 1))
         go.start()
-        g_xy.append(go)
-    for p in range(pieces // 2, pieces):
-        sum_x(p)
-    for p in range(pieces // 2):
-        sum_z(p)
-    for n, d in enumerate(plane):
-        part = g_all.at[c, lax.rem(x - d[0] + nx, nx), lax.rem(y - d[1] + ny, ny)]
-        copy(part, part, xy_s.at[n], xy_r.at[n], hop("xy", d)).wait_recv()
+        g_core_go.append(go)
     pending += g_xy
-    g_gc = copy(g_all.at[c], g_all.at[c], core_s.at[1], core_r.at[1], hop("core", 1))
-    g_gc.start()
-    for p in range(pieces // 2, pieces):
-        sum_z(p)
-    copy(g_all.at[other], g_all.at[other], core_s.at[1], core_r.at[1], hop("core", 1)).wait_recv()
-    pending += [g_gc]
-
-    nb = rank // 128
+    sum_z(3)
+    gather_x(1)
+    for h, part in enumerate(parts):
+        half_sem = [1, 2 + 2 * pieces][h]
+        theirs = g_all.at[other, :, :, part]
+        copy(theirs, theirs, core_s.at[half_sem], core_r.at[half_sem], hop("core", 1)).wait_recv()
+    pending += g_core_go
+
     gr = g_all.shape[3] * g_all.shape[4]
     for i in range(2):
         for j in range(nx):
             for k in range(ny):
                 lo = (i * nx + j) * gr
                 m[lo:lo + gr, gcols * k:gcols * (k + 1)] = g_all[i, j, k].reshape(gr, gcols)
-    row = lax.broadcasted_iota(jnp.int32, (128, 128), 0)
-    col = lax.broadcasted_iota(jnp.int32, (128, 128), 1)
-    eye = jnp.where(row == col, 1.0, 0.0)
-    for i in range(nb):
-        for j in range(nb):
-            m[128 * i:128 * (i + 1), rank + 128 * j:rank + 128 * (j + 1)] = eye if i == j else jnp.zeros_like(eye)
-    stages = [(gather_x, p) for p in range(pieces)] + [(gather_core, p) for p in range(pieces)]
-    first = (2, 4, 12, 20, 36, 44, 52, 60)
-    plan = {at_step * nb // 4: stage for at_step, stage in zip(first, stages)}
-    assert len(plan) == len(stages)
+    plan = {3: (gather_x, 2), 8: (gather_core, 0), 14: (gather_x, 3), 20: (gather_core, 1),
+            30: (gather_core, 2), 42: (gather_core, 3)}
+    plan = {at_step * nb // 4: stage for at_step, stage in plan.items()}
+    assert len(plan) == 6 and pieces == 4
     for k in range(nb):
         lo, hi = 128 * k, 128 * (k + 1)
         w[:, 0:128] = m[lo:hi, lo:hi]
@@ -289,20 +303,26 @@
             m[hi:, hi:rank + hi] = m[hi:, hi:rank + hi] - dot(
                 m[lo:hi, hi:rank], m[lo:hi, hi:rank + hi], ((0,), (0,)), HIGHEST)
     high, low = split(m[:, rank:])
-    orth_ref[...] = (dot(p_all, high, ((1,), (1,))) + dot(p_all, low, ((1,), (1,)))).astype(BF16)
+    both = jnp.concatenate([high, low], axis=0)
     for p in range(pieces):
         got_core(p)
 
-    ones = jnp.ones((8, cb), F32)
-    total = jnp.zeros((8, rank), F32)
+    total = jnp.zeros((rank, 128), F32)
     for k in range(nz):
-        t = t_all[:, :, :, k].reshape(rank, cb)
-        r = dot(high, t) + dot(low, t)
-        r_ref[:, cb * k:cb * (k + 1)] = r.astype(BF16)
+        r = dot(both, t_all[:, :, :, k].reshape(rank, cb))
+        r = r[:rank] + r[rank:]
         r_f32[:, cb * k:cb * (k + 1)] = r
-        total = total + dot(ones, r * r, ((1,), (1,)), HIGHEST)
-    sq_own[...] = total
+        for i in range(cb // 128):
+            part = r[:, 128 * i:128 * (i + 1)]
+            total = total + part * part
+    sq_own[...] = dot(jnp.ones((8, 128), F32), total, ((1,), (1,)), HIGHEST)
     sq_go = start_exchange("y", 4, sq_own, sq_rx, ys)
+    orth = (dot(p_all, high, ((1,), (1,))) + dot(p_all, low, ((1,), (1,)))).astype(BF16)
+    orth_ref[...] = orth
+    for k in range(nz):
+        place = pl.ds(cb * k, cb)
+        low_rank = dot(orth, r_f32[:, place].astype(BF16))
+        mom_ref[:, place] = (buf[:, :, place].reshape(rows, cb).astype(F32) - 0.05 * low_rank).astype(BF16)
     arrived(sq_go)
     total = sum((sq_rx[d] for d in range(ny - 1)), sq_own[...])
     scale = lax.rsqrt(total / cols_total + 1e-06)
@@ -329,13 +349,13 @@
         functools.partial(update_kernel, shape, cols_total),
         out_shape=(
             vmem((rows, rank), BF16),
+            vmem((rows, cols), BF16),
             vmem((rank, cols), BF16),
-            vmem((rank, cols), BF16),
-            vmem((ny, part, cols), BF16),
         ),
         in_specs=[hbm] * 3,
-        out_specs=(space,) * 4,
+        out_specs=(space,) * 3,
         scratch_shapes=[
+            vmem((ny, part, cols), BF16),
             vmem((ny, part, cols), BF16),
             vmem((ny, part, cols), BF16),
             vmem((cols, rank), BF16),
@@ -366,11 +386,11 @@
             vmem((8, rank), F32),
             vmem((ny - 1, 8, rank), F32),
             sem((3, ny)),
-            sem((2 + 2 * np,)), sem((2 + 2 * np,)),
+            sem((3 + 2 * np,)), sem((3 + 2 * np,)),
             sem((1 + 2 * np, nx - 1)), sem((1 + 2 * np, nx - 1)),
             sem((5, ny - 1)), sem((5, ny - 1)),
-            sem((1 + 2 * np, nz - 1)), sem((1 + 2 * np, nz - 1)),
-            sem((nx * ny - 1,)), sem((nx * ny - 1,)),
+            sem((2 + 2 * np, nz - 1)), sem((2 + 2 * np, nz - 1)),
+            sem((2, nx * ny - 1)), sem((2, nx * ny - 1)),
         ],
         compiler_params=pltpu.CompilerParams(
             collective_id=0, has_side_effects=True, vmem_limit_bytes=VMEM_LIMIT),
@@ -469,22 +489,19 @@
     return high, (x - high.astype(F32)).astype(BF16)
 
 
-def outputs_kernel(orth, buf, r_t, nb_t, mom_hbm, basis_hbm, dir_hbm, mom_out, basis_out, dir_out, sems):
-    blocks, rows, wide = mom_out.shape
+def outputs_kernel(orth, new_mom, nb_t, mom_hbm, basis_hbm, dir_hbm, basis_out, dir_out, sems):
+    blocks, rows, wide = dir_out.shape
     factor = orth[...]
-    copies = []
+    copies = [pltpu.make_async_copy(new_mom, mom_hbm, sems.at[2, 0])]
+    copies[0].start()
     for i in range(blocks):
         place = pl.ds(i * wide, wide)
-        low_rank = dot(factor, r_t[:, place])
-        mine = buf[:, :, place].reshape(rows, wide)
-        mom_out[i] = (mine.astype(F32) - 0.05 * low_rank).astype(BF16)
         new_basis = nb_t[:, place]
+        dir_out[i] = (math.sqrt(ROWS / RANK) * dot(factor, new_basis)).astype(BF16)
         basis_out[place, :] = new_basis.T
-        dir_out[i] = (math.sqrt(ROWS / RANK) * dot(factor, new_basis)).astype(BF16)
         for n, (src, dst) in enumerate((
-            (mom_out.at[i], mom_hbm.at[:, place]),
+            (dir_out.at[i], dir_hbm.at[:, place]),
             (basis_out.at[place, :], basis_hbm.at[place, :]),
-            (dir_out.at[i], dir_hbm.at[:, place]),
         )):
             go = pltpu.make_async_copy(src, dst, sems.at[n, i])
             go.start()
@@ -493,14 +510,14 @@
         go.wait()
 
 
-def outputs_call(orth, buf, r_t, nb_t):
-    rows, cols = buf.shape[0] * buf.shape[1], buf.shape[2]
+def outputs_call(orth, new_mom, nb_t):
+    rows, cols = new_mom.shape
     rank = orth.shape[1]
     wide = 256
     blocks = cols // wide
     space = pl.BlockSpec(memory_space=pltpu.VMEM)
     hbm = pl.BlockSpec(memory_space=pl.ANY)
-    args = [pltpu.with_memory_space_constraint(v, pltpu.VMEM) for v in (orth, buf, r_t, nb_t)]
+    args = [pltpu.with_memory_space_constraint(v, pltpu.VMEM) for v in (orth, new_mom, nb_t)]
     return pl.pallas_call(
         outputs_kernel,
         out_shape=(
@@ -508,10 +525,9 @@
             jax.ShapeDtypeStruct((cols, rank), BF16),
             jax.ShapeDtypeStruct((rows, cols), BF16),
         ),
-        in_specs=[space] * 4,
+        in_specs=[space] * 3,
         out_specs=(hbm,) * 3,
         scratch_shapes=[
-            pltpu.VMEM((blocks, rows, wide), BF16),
             pltpu.VMEM((cols, rank), BF16),
             pltpu.VMEM((blocks, rows, wide), BF16),
             pltpu.SemaphoreType.DMA((3, blocks)),
@@ -522,8 +538,8 @@
 
 
 def per_device(momentum, gradient, old_basis):
-    orth, r_t, nb_t, buf = update_call(SHAPE, COLS, momentum, gradient, old_basis)
-    return outputs_call(orth, buf, r_t, nb_t)
+    orth, new_momentum, basis_t = update_call(SHAPE, COLS, momentum, gradient, old_basis)
+    return outputs_call(orth, new_momentum, basis_t)
 
 
 def solution(mesh):

time: 86.5 us -> 80.4 us (0.929)
  Pallas kernels: 85.6 us -> 79.5 us
    pallas_call x1, Pallas kernels: 82.5 us -> 76.8 us  [update_call(): pl.pallas_call(functools.partial(update_kernel, shape, cols_total), out_s...]
where the time goes in v4:
time: 80.4 us; the launch traced here: 80.3 us
  Pallas kernels  79.5 us (99%)
    pallas_call x1, Pallas kernels, update_call(): pl.pallas_call(functools.partial(update_kernel, shape, cols_total), out_s...  76.8 us
    pallas_call x1, Pallas kernels, outputs_call(): pl.pallas_call(outputs_kernel, out_shape=(jax.ShapeDtypeStruct((rows, col...  2.69 us

profile of v4, /device:TPU:1, one launch (start us, length us, event | category | flops | bytes accessed | tf_op | source)
XLA Modules:
  0.0 80.3 jit_solution(3387425070973880955)
XLA Ops:
  0.6 76.8 %update.1 = (bf16[448,512]{1,0:T(8,128)(2,1)S(1)}, bf16[448,2048]{1,0:T(8,128)(2,1)S(1)}, bf16[512,2048]{1,0:T(8,128)(2,1)S(1)}) custom-call(bf16[4,112,2048]{2,1,0:T(8,128)(2,1)} %bitcast.2, bf16[4,112,2048]{2,1,0:T(8,128)(2,1)} %bitcast.3, bf16[2048,512]{1,0:T(8,128)(2,1)} %basis_hbm.1), custom_call_target="tpu_custom_call" | custom-call | tf_op jit(solution)/shard_map/update/pallas_call | solution.py:348
  77.5 2.7 %outputs.1 = (bf16[448,2048]{1,0:T(8,128)(2,1)}, bf16[2048,512]{1,0:T(8,128)(2,1)}, bf16[448,2048]{1,0:T(8,128)(2,1)}) custom-call(bf16[448,512]{1,0:T(8,128)(2,1)S(1)} %get-tuple-element.6.orth, bf16[448,2048]{1,0:T(8,128)(2,1)S(1)} %get-tuple-element.7.new_mom, bf16[512,2048]{1,0:T(8,128)(2,1)S(1)} %get-tuple-element.8.nb_t), custom_call_target="tpu_custom_call" | custom-call | tf_op jit(solution)/shard_map/outputs/pallas_call | solution.py:521

commit v5 on v4

--- a/solution.py
+++ b/solution.py
@@ -137,7 +137,8 @@
         p_part[d - 1] = partial_rows(d).astype(BF16)
     pl.semaphore_wait(barrier, len(peers))
     rank = p_sum.shape[2]
-    sides = [pl.ds(0, rank // 2), pl.ds(rank // 2, rank // 2)]
+    quarter = rank // 4
+    sides = [pl.ds(n * quarter, quarter) for n in range(4)]
     p_go = []
     for n, side in enumerate(sides):
         p_go.append([])
@@ -150,13 +151,13 @@
     p_gather = []
     for n, side in enumerate(sides):
         arrived(p_go[n])
-        total = own[:, n * rank // 2:(n + 1) * rank // 2]
+        total = own[:, n * quarter:(n + 1) * quarter]
         for d in y_order[:-1]:
             total = total + p_rx[d - 1, :, side].astype(F32)
         p_sum[y, :, side] = total.astype(BF16)
-        p_gather.append(start_gather("y", 2 + n, lambda i: p_sum.at[i, :, side], ys))
+        p_gather.append(start_gather("y", 4 + n, lambda i: p_sum.at[i, :, side], ys))
     for n, side in enumerate(sides):
-        gathered("y", 2 + n, lambda i: p_sum.at[i, :, side], p_gather[n], ys)
+        gathered("y", 4 + n, lambda i: p_sum.at[i, :, side], p_gather[n], ys)
 
     rows = buf.shape[0] * buf.shape[1]
     half = rank // 2
@@ -288,8 +289,8 @@
             for k in range(ny):
                 lo = (i * nx + j) * gr
                 m[lo:lo + gr, gcols * k:gcols * (k + 1)] = g_all[i, j, k].reshape(gr, gcols)
-    plan = {3: (gather_x, 2), 8: (gather_core, 0), 14: (gather_x, 3), 20: (gather_core, 1),
-            30: (gather_core, 2), 42: (gather_core, 3)}
+    plan = {12: (gather_x, 2), 20: (gather_x, 3), 30: (gather_core, 0), 40: (gather_core, 1),
+            52: (gather_core, 2), 62: (gather_core, 3)}
     plan = {at_step * nb // 4: stage for at_step, stage in plan.items()}
     assert len(plan) == 6 and pieces == 4
     for k in range(nb):
@@ -316,7 +317,7 @@
             part = r[:, 128 * i:128 * (i + 1)]
             total = total + part * part
     sq_own[...] = dot(jnp.ones((8, 128), F32), total, ((1,), (1,)), HIGHEST)
-    sq_go = start_exchange("y", 4, sq_own, sq_rx, ys)
+    sq_go = start_exchange("y", 8, sq_own, sq_rx, ys)
     orth = (dot(p_all, high, ((1,), (1,))) + dot(p_all, low, ((1,), (1,)))).astype(BF16)
     orth_ref[...] = orth
     for k in range(nz):
@@ -388,7 +389,7 @@
             sem((3, ny)),
             sem((3 + 2 * np,)), sem((3 + 2 * np,)),
             sem((1 + 2 * np, nx - 1)), sem((1 + 2 * np, nx - 1)),
-            sem((5, ny - 1)), sem((5, ny - 1)),
+            sem((9, ny - 1)), sem((9, ny - 1)),
             sem((2 + 2 * np, nz - 1)), sem((2 + 2 * np, nz - 1)),
             sem((2, nx * ny - 1)), sem((2, nx * ny - 1)),
         ],
@@ -442,16 +443,32 @@
     return dot(left, jnp.concatenate([right_a, right_v], axis=1).astype(BF16), ((0,), (0,)))
 
 
+def times_inverse(cols, inv):
+    out = []
+    for k in range(8):
+        acc = cols[0] * inv[k][0]
+        for j in range(1, k + 1):
+            acc = acc + cols[j] * inv[k][j]
+        out.append(acc)
+    return out
+
+
 def factor128(r, between):
     sub = lax.broadcasted_iota(jnp.int32, (8, 128), 0)
     a, v = r[0:8, 0:128], r[0:8, 128:256]
     cols = [lanes(a, k) for k in range(8)]
+    last = None
     for s in range(16):
         if s in between:
             between[s][0](between[s][1])
         lo = 8 * s
         if s < 15:
             an, vn = r[lo + 8:lo + 16, 0:128], r[lo + 8:lo + 16, 128:256]
+            if last is not None:
+                low = times_inverse([lanes(an, lo - 8 + k) for k in range(8)], last[0])
+                for k in range(8):
+                    an = an - low[k] * rows8(last[1], k)
+                    vn = vn - low[k] * rows8(last[2], k)
             below = [lanes(an, lo + k) for k in range(8)]
             ahead = [lanes(an, lo + 8 + k) for k in range(8)]
         inv = factor8(cols)
@@ -465,12 +482,7 @@
             new_v = tv if new_v is None else new_v + tv
         r[lo:lo + 8, 128:256] = new_v
         if s < 15:
-            low = []
-            for k in range(8):
-                acc = below[0] * inv[k][0]
-                for j in range(1, k + 1):
-                    acc = acc + below[j] * inv[k][j]
-                low.append(acc)
+            low = times_inverse(below, inv)
             cols = []
             for k in range(8):
                 an = an - low[k] * rows8(new_a, k)
@@ -480,8 +492,9 @@
                     acc = acc - low[j] * rows8(low[j], k)
                 cols.append(acc)
             a, v = an, vn
-        if s < 14:
-            r[lo + 16:128, :] = r[lo + 16:128, :] - rank8(new_a, new_v)[lo + 16:128, :]
+        last = inv, new_a, new_v
+        if s < 13:
+            r[lo + 24:128, :] = r[lo + 24:128, :] - rank8(new_a, new_v)[lo + 24:128, :]
 
 
 def split(x):

time: 80.4 us -> 77.8 us (0.968)
  Pallas kernels: 79.5 us -> 76.9 us
    pallas_call x1, Pallas kernels: 76.8 us -> 74.2 us  [update_call(): pl.pallas_call(functools.partial(update_kernel, shape, cols_total), out_s...]
where the time goes in v5:
time: 77.8 us; the launch traced here: 77.7 us
  Pallas kernels  76.9 us (99%)
  between operations  0.8 us (1%)
    pallas_call x1, Pallas kernels, update_call(): pl.pallas_call(functools.partial(update_kernel, shape, cols_total), out_s...  74.2 us
    pallas_call x1, Pallas kernels, outputs_call(): pl.pallas_call(outputs_kernel, out_shape=(jax.ShapeDtypeStruct((rows, col...  2.69 us

profile of v5, /device:TPU:1, one launch (start us, length us, event | category | flops | bytes accessed | tf_op | source)
XLA Modules:
  0.0 77.7 jit_solution(6307136382572355245)
XLA Ops:
  0.6 74.2 %update.1 = (bf16[448,512]{1,0:T(8,128)(2,1)S(1)}, bf16[448,2048]{1,0:T(8,128)(2,1)S(1)}, bf16[512,2048]{1,0:T(8,128)(2,1)S(1)}) custom-call(bf16[4,112,2048]{2,1,0:T(8,128)(2,1)} %bitcast.2, bf16[4,112,2048]{2,1,0:T(8,128)(2,1)} %bitcast.3, bf16[2048,512]{1,0:T(8,128)(2,1)} %basis_hbm.1), custom_call_target="tpu_custom_call" | custom-call | tf_op jit(solution)/shard_map/update/pallas_call | solution.py:349
  74.9 2.7 %outputs.1 = (bf16[448,2048]{1,0:T(8,128)(2,1)}, bf16[2048,512]{1,0:T(8,128)(2,1)}, bf16[448,2048]{1,0:T(8,128)(2,1)}) custom-call(bf16[448,512]{1,0:T(8,128)(2,1)S(1)} %get-tuple-element.6.orth, bf16[448,2048]{1,0:T(8,128)(2,1)S(1)} %get-tuple-element.7.new_mom, bf16[512,2048]{1,0:T(8,128)(2,1)S(1)} %get-tuple-element.8.nb_t), custom_call_target="tpu_custom_call" | custom-call | tf_op jit(solution)/shard_map/outputs/pallas_call | solution.py:534
